TPU v7x, 512 devices: a whole 4x8x8 slice. The times are simulated.
512 devices in a mesh: row: 16 (over z, x_hi), col: 32 (over y, x_lo, core).
Axes of the slice: x: 4 (x_hi: 2, x_lo: 2; x = x_hi * 2 + x_lo), y: 8, z: 8, core: 2. Of those that a mesh axis runs over, the one named last changes fastest.
Arguments:
- tokens: bfloat16 [1024, 8192], P('col', 'row'), may hold values from -6 to 6
- out_grad: bfloat16 [1024, 8192], P('col', 'row'), may hold values from -4 to 4
- gate_weight: bfloat16 [8192, 16384], P('row', 'col'), may hold values from -0.0625 to 0.0625
- up_weight: bfloat16 [8192, 16384], P('row', 'col'), may hold values from -0.0625 to 0.0625
- down_weight: bfloat16 [16384, 8192], P('col', 'row'), may hold values from -0.046875 to 0.046875
Outputs:
- in_grad: bfloat16 [1024, 8192], P('col', 'row')
- gate_wgrad: bfloat16 [8192, 16384], P('row', 'col')
- up_wgrad: bfloat16 [8192, 16384], P('row', 'col')
- down_wgrad: bfloat16 [16384, 8192], P('col', 'row')
All inputs are finite; a program needn't handle non-finite values.
Results may differ from a plain program's by a relative error of at most 0.0049.
Values may be sent and summed in bfloat16 or wider, within the bound.
No kernel may reach another device: no remote copies, remote signals or barrier semaphores. Data moves between devices by JAX's collectives and lax.ppermute only.
A program may use at most 64 MiB of HBM per device.

v0:
```python
import jax
import jax.numpy as jnp
from jax import lax
from jax.sharding import PartitionSpec as P


def swiglu_back(gate, up, hidden_grad):
    sig = jax.nn.sigmoid(gate)
    act = gate * sig
    hidden = (act * up).astype(jnp.bfloat16)
    gate_grad = (hidden_grad * up * sig * (1.0 + gate * (1.0 - sig))).astype(jnp.bfloat16)
    up_grad = (hidden_grad * act).astype(jnp.bfloat16)
    return (hidden, gate_grad, up_grad)


def contract_rows(left, right):
    return lax.dot_general(
        left, right, (((0,), (0,)), ((), ())), preferred_element_type=jnp.float32
    )


def contract_cols(left, right):
    return lax.dot_general(
        left, right, (((1,), (1,)), ((), ())), preferred_element_type=jnp.float32
    )


def per_device(tokens, out_grad, gate_weight, up_weight, down_weight):
    inputs = lax.all_gather(tokens, "col", axis=0, tiled=True)
    grads = lax.all_gather(out_grad, "col", axis=0, tiled=True)
    gate_part = jnp.dot(inputs, gate_weight, preferred_element_type=jnp.float32)
    up_part = jnp.dot(inputs, up_weight, preferred_element_type=jnp.float32)
    hidden_part = contract_cols(grads, down_weight)
    gate, up, hidden_grad = lax.psum((gate_part, up_part, hidden_part), "row")
    hidden, gate_grad, up_grad = swiglu_back(gate, up, hidden_grad)
    down_wgrad = contract_rows(hidden, grads).astype(jnp.bfloat16)
    gate_wgrad = contract_rows(inputs, gate_grad).astype(jnp.bfloat16)
    up_wgrad = contract_rows(inputs, up_grad).astype(jnp.bfloat16)
    in_grad = lax.psum_scatter(
        contract_cols(gate_grad, gate_weight) + contract_cols(up_grad, up_weight),
        "col",
        scatter_dimension=0,
        tiled=True,
    ).astype(jnp.bfloat16)
    return (in_grad, gate_wgrad, up_wgrad, down_wgrad)


def solution(mesh):
    in_specs = (P("col", "row"), P("col", "row"), P("row", "col"), P("row", "col"), P("col", "row"))
    out_specs = (P("col", "row"), P("row", "col"), P("row", "col"), P("col", "row"))
    return jax.shard_map(
        per_device, mesh=mesh, in_specs=in_specs, out_specs=out_specs, check_vma=False
    )
```

profile of v0, /device:TPU:4, one launch (start us, length us, event | category | flops | bytes accessed | tf_op | source)
XLA Modules:
  0.0 586.1 jit_solution(1390557399773833050)
XLA Ops:
  7.2 0.0 all-gather.5.cloned.1.call-start
  7.2 0.7 all-gather.5.cloned.1.call-update
  7.9 0.0 all-gather.3.cloned.1.call-start
  8.0 0.7 all-gather.3.cloned.1.call-update
  8.7 0.0 all-reduce.3.cloned.1.call-start
  8.7 72.0 %all-gather.5.cloned.1.call-done = bf16[1024,512]{1,0:T(8,128)(2,1)} async-done(((bf16[32,512]{1,0:T(8,128)(2,1)}), bf16[1024,512]{1,0:T(8,128)(2,1)}) %all-gather.5.cloned.1.call-update) | async-done | bytes 1048592 | tf_op jit(solution)/shard_map/all_gather | solution.py:29
  80.7 3.4 fusion.7
  84.1 2.0 fusion.6
  86.1 62.9 %all-gather.3.cloned.1.call-done = bf16[1024,512]{1,0:T(8,128)(2,1)} async-done(((bf16[32,512]{1,0:T(8,128)(2,1)}), bf16[1024,512]{1,0:T(8,128)(2,1)}) %all-gather.3.cloned.1.call-update) | async-done | bytes 1048592 | tf_op jit(solution)/shard_map/all_gather | solution.py:30
  149.0 3.3 fusion.5
  152.3 0.0 all-reduce.3.cloned.1.call-update
  152.4 0.0 reduce-scatter.2.cloned.1.call-start
  152.4 293.1 %all-reduce.3.cloned.1.call-done = (f32[1024,512]{1,0:T(8,128)}, f32[1024,512]{1,0:T(8,128)}, f32[1024,512]{1,0:T(8,128)}) async-done(((f32[1024,512]{1,0:T(8,128)}, f32[1024,512]{1,0:T(8,128)}, f32[1024,512]{1,0:T(8,128)}), (f32[1024,512]{1,0:T(8,128)}, f32[1024,512]{1,0:T(8,128)}, f32[1024,512]{1,0:T(8,128)})) %all-reduce.3.cloned.1.call-update) | async-done | bytes 6291472 | tf_op jit(solution)/shard_map/psum | solution.py:34
  445.5 4.0 multiply_convert_fusion.1
  449.5 0.7 fusion.8
  450.3 0.3 copy-done.2
  450.5 2.1 convolution_add_fusion
  452.7 0.7 fusion.1
  453.4 1.0 copy.9
  454.4 2.0 fusion.2
  456.5 1.0 copy.10
  457.5 3.8 convolution_convert_fusion
  461.3 116.8 %reduce-scatter.2.cloned.1.call-done = f32[32,512]{1,0:T(8,128)} async-done(((f32[1024,512]{1,0:T(8,128)}), f32[32,512]{1,0:T(8,128)}) %reduce-scatter.2.cloned.1.call-update) | async-done | bytes 65552 | tf_op jit(solution)/shard_map/reduce_scatter | solution.py:39
  578.1 1.5 convert_element_type.29
  (12 shorter events, 0.0 us)
Async XLA Ops:
  7.2 73.5 %copy-start = (bf16[512,512]{1,0:T(8,128)(2,1)S(1)}, bf16[512,512]{1,0:T(8,128)(2,1)}, u32[]{:S(2)}) copy-start(bf16[512,512]{1,0:T(8,128)(2,1)} %param.7) | copy-start | bytes 1572868
  7.2 76.9 %copy-start.3 = (bf16[512,512]{1,0:T(8,128)(2,1)S(1)}, bf16[512,512]{1,0:T(8,128)(2,1)}, u32[]{:S(2)}) copy-start(bf16[512,512]{1,0:T(8,128)(2,1)} %param.8) | copy-start | bytes 1572868
  7.2 73.5 %all-gather.5.cloned.1.call-start = ((), (), s32[]{:S(2)}) async-start(), calls=%async_computation.2 | async-start | bytes 1081344 | tf_op jit(solution)/shard_map/all_gather | solution.py:29
  7.9 141.1 %all-gather.3.cloned.1.call-start = ((), (), s32[]{:S(2)}) async-start(), calls=%async_computation.1 | async-start | bytes 1081344 | tf_op jit(solution)/shard_map/all_gather | solution.py:30
  8.7 436.8 %all-reduce.3.cloned.1.call-start = ((), (), s32[]{:S(2)}) async-start(), calls=%async_computation.4 | async-start | bytes 12582912 | tf_op jit(solution)/shard_map/psum | solution.py:34
  80.7 3.4 copy-start.1
  84.1 64.9 %copy-start.5 = (bf16[512,512]{1,0:T(8,128)(2,1)S(1)}, bf16[512,512]{1,0:T(8,128)(2,1)}, u32[]{:S(2)}) copy-start(bf16[512,512]{1,0:T(8,128)(2,1)} %param.9) | copy-start | bytes 1572868
  152.4 425.8 %reduce-scatter.2.cloned.1.call-start = ((), (), s32[]{:S(2)}) async-start(), calls=%async_computation.3 | async-start | bytes 2162688 | tf_op jit(solution)/shard_map/reduce_scatter | solution.py:39
  449.5 1.0 copy-start.2
  454.4 3.1 copy-start.4
Sparse Core Ops, SparseCore 0:
  10.2 70.4 all-gather.4
  82.8 66.1 all-gather.2
  152.5 292.9 all-reduce.2
  452.8 125.2 reduce-scatter.1
where the time goes:
time: 586 us
  waiting for transfers between devices  546 us (93%)
  matrix products  18.1 us (3%)
  between operations  13.8 us (2%)
    psum x1, waiting for transfers between devices, per_device(): gate, up, hidden_grad = lax.psum((gate_part, up_part, hidden_part), 'row')  293 us
    reduce_scatter x1, waiting for transfers between devices, per_device(): lax.psum_scatter(contract_cols(gate_grad, gate_weight) + contract_cols(up...  117 us
    all_gather x1, waiting for transfers between devices, per_device(): inputs = lax.all_gather(tokens, 'col', axis=0, tiled=True)  72 us
    all_gather x1, waiting for transfers between devices, per_device(): grads = lax.all_gather(out_grad, 'col', axis=0, tiled=True)  62.9 us
  transfers between devices with their start and end apart: 4, of which 4 were waited for; matrix products, arithmetic and copies ran while one was open for 2% of the time, Pallas kernels for 0%

commit v1 on v0

v1 whole, which is shorter than its diff:
```python
import jax
import jax.numpy as jnp
from jax import lax
from jax.sharding import Mesh, PartitionSpec as P

ROW = ("zh", "zl", "xh")
COL = ("y", "xl", "c")
WEIGHT_BOUND = 0.0625
DOWN_BOUND = 0.046875


def swiglu_back(gate, up, hidden_grad):
    sig = jax.nn.sigmoid(gate)
    act = gate * sig
    hidden = (act * up).astype(jnp.bfloat16)
    gate_grad = (hidden_grad * up * sig * (1.0 + gate * (1.0 - sig))).astype(jnp.bfloat16)
    up_grad = (hidden_grad * act).astype(jnp.bfloat16)
    return (hidden, gate_grad, up_grad)


def contract_rows(left, right):
    return lax.dot_general(
        left, right, (((0,), (0,)), ((), ())), preferred_element_type=jnp.float32
    )


def contract_cols(left, right):
    return lax.dot_general(
        left, right, (((1,), (1,)), ((), ())), preferred_element_type=jnp.float32
    )


def matmul(left, right):
    return jnp.dot(left, right, preferred_element_type=jnp.float32)


def swap(x, axis):
    return lax.ppermute(x, axis, [(0, 1), (1, 0)])


def scale_exponent(x, weight_bound, depth):
    top = jnp.max(jnp.abs(x)).astype(jnp.float32)
    bound = jnp.maximum(top, 1e-30) * (weight_bound * depth)
    return jnp.clip(jnp.floor(14.0 - jnp.log2(bound)), -100.0, 100.0)


def per_device(zh_size, blocks, tokens, out_grad, gate_weight, up_weight, down_weight):
    zl = lax.axis_index("zl")
    xh = lax.axis_index("xh")
    rows, depth = tokens.shape
    ff = gate_weight.shape[1]

    near = jnp.concatenate([gate_weight, up_weight, down_weight], axis=0)
    far = swap(near, "zl")
    far_gate, far_up, far_down = far[:depth], far[depth : 2 * depth], far[2 * depth :]

    shard = jnp.concatenate([tokens, out_grad], axis=1)
    own = lax.all_to_all(
        jnp.broadcast_to(shard[None], (blocks, rows, 2 * depth)), ("y", "xl"), 0, 0, tiled=True
    )
    own = own.reshape(zh_size // 2, 2, -1, 2 * depth)
    first = zl == 0
    mine = jnp.where(first, own[:, 0], own[:, 1])
    theirs = jnp.where(first, own[:, 1], own[:, 0])
    ext = swap(theirs, "zl").reshape(-1, 2 * depth)
    own = own.reshape(-1, 2 * depth)
    other = swap(own, "c")
    ext_other = swap(ext, "c")
    other_halves = other.reshape(zh_size // 2, 2, -1, 2 * depth)
    mine_other = jnp.where(first, other_halves[:, 0], other_halves[:, 1])
    every = jnp.concatenate([own, other], axis=0)
    near_half = jnp.concatenate([mine, mine_other], axis=0).reshape(-1, 2 * depth)
    far_half = jnp.concatenate([ext, ext_other], axis=0)
    inputs, grads = every[:, :depth], every[:, depth:]

    gate_part = matmul(near_half[:, :depth], gate_weight) + matmul(far_half[:, :depth], far_gate)
    up_part = matmul(near_half[:, :depth], up_weight) + matmul(far_half[:, :depth], far_up)
    hidden_part = contract_cols(near_half[:, depth:], down_weight) + contract_cols(
        far_half[:, depth:], far_down
    )

    both = jnp.concatenate([near_half, far_half], axis=1).reshape(-1, 2, 2, depth)
    exp_in = scale_exponent(both[:, :, 0], WEIGHT_BOUND, 2 * depth)
    exp_grad = scale_exponent(both[:, :, 1], DOWN_BOUND, 2 * depth)
    half = near_half.shape[0]
    parts = jnp.concatenate(
        [
            gate_part * jnp.exp2(exp_in),
            up_part * jnp.exp2(exp_in),
            hidden_part * jnp.exp2(exp_grad),
            jnp.full((half, 64), exp_in, jnp.float32),
            jnp.full((half, 64), exp_grad, jnp.float32),
        ],
        axis=1,
    ).astype(jnp.float16)
    group = 2 * zh_size
    parts = parts.reshape(group, half // group, -1)
    parts = lax.all_to_all(parts, ("zh", "xh"), 0, 0, tiled=True).astype(jnp.float32)
    in_scale = jnp.exp2(-parts[:, :1, 3 * ff : 3 * ff + 1])
    grad_scale = jnp.exp2(-parts[:, :1, 3 * ff + 64 : 3 * ff + 65])
    gate = jnp.sum(parts[:, :, :ff] * in_scale, axis=0)
    up = jnp.sum(parts[:, :, ff : 2 * ff] * in_scale, axis=0)
    hidden_grad = jnp.sum(parts[:, :, 2 * ff : 3 * ff] * grad_scale, axis=0)
    trio = jnp.concatenate(swiglu_back(gate, up, hidden_grad), axis=1)

    beside = swap(trio, "xh")
    pair = jnp.concatenate(
        [jnp.where(xh == 0, trio, beside), jnp.where(xh == 0, beside, trio)], axis=0
    )
    trio = lax.all_gather(pair, ("zh", "zl"), axis=0, tiled=True)
    hidden, gate_grad, up_grad = trio[:, :ff], trio[:, ff : 2 * ff], trio[:, 2 * ff :]

    in_part = contract_cols(gate_grad, gate_weight) + contract_cols(up_grad, up_weight)
    share = in_part.shape[0] // 2
    in_part = in_part[:share] + swap(in_part[share:], "c")
    in_part = lax.all_to_all(
        in_part.astype(jnp.bfloat16).reshape(blocks, rows, depth), ("y", "xl"), 0, 0, tiled=True
    )
    in_grad = jnp.sum(in_part.astype(jnp.float32), axis=0).astype(jnp.bfloat16)

    down_wgrad = contract_rows(hidden, grads).astype(jnp.bfloat16)
    gate_wgrad = contract_rows(inputs, gate_grad).astype(jnp.bfloat16)
    up_wgrad = contract_rows(inputs, up_grad).astype(jnp.bfloat16)
    return (in_grad, gate_wgrad, up_wgrad, down_wgrad)


def solution(mesh):
    row, col = mesh.devices.shape
    zh_size, y_size = row // 4, col // 4
    fine = Mesh(
        mesh.devices.reshape(zh_size, 2, 2, y_size, 2, 2), ("zh", "zl", "xh", "y", "xl", "c")
    )

    def body(*args):
        return per_device(zh_size, 2 * y_size, *args)

    in_specs = (P(COL, ROW), P(COL, ROW), P(ROW, COL), P(ROW, COL), P(COL, ROW))
    out_specs = (P(COL, ROW), P(ROW, COL), P(ROW, COL), P(COL, ROW))
    return jax.shard_map(
        body, mesh=fine, in_specs=in_specs, out_specs=out_specs, check_vma=False
    )
```

time: 586 us -> 267 us (0.46)
  waiting for transfers between devices: 546 us -> 124 us
  blocking collectives: 0 us -> 47.7 us
  starting transfers between devices: 0.16 us -> 31.5 us
  other arithmetic: 5.48 us -> 16.8 us
  local copies, waits for them, and re-layouts: 2.29 us -> 9.15 us
    psum x1 -> x0, waiting for transfers between devices: 293 us -> none  [per_device(): gate, up, hidden_grad = lax.psum((gate_part, up_part, hidden_part), 'row')]
    reduce_scatter x1 -> x0, waiting for transfers between devices: 117 us -> none  [per_device(): lax.psum_scatter(contract_cols(gate_grad, gate_weight) + contract_cols(up...]
    all_gather x2 -> x1, waiting for transfers between devices: 135 us -> 48.2 us  [per_device(): trio = lax.all_gather(pair, ('zh', 'zl'), axis=0, tiled=True)]
    all_to_all x0 -> x1, blocking collectives: none -> 47.7 us  [per_device(): lax.all_to_all(parts, ('zh', 'xh'), 0, 0, tiled=True).astype(jnp.float32)]
    all_to_all x0 -> x2, waiting for transfers between devices: none -> 38.3 us  [the longest x1 28.6 us: per_device(): lax.all_to_all(jnp.broadcast_to(shard[None], (blocks, rows, 2 * depth)),...]
    ppermute x0 -> x6, waiting for transfers between devices: none -> 37.9 us  [swap(): return lax.ppermute(x, axis, [(0, 1), (1, 0)])]
    ppermute x0 -> x6, starting transfers between devices: none -> 16.1 us  [swap(): return lax.ppermute(x, axis, [(0, 1), (1, 0)])]
    all_to_all x0 -> x2, starting transfers between devices: none -> 15.4 us  [the longest x1 7.97 us: per_device(): lax.all_to_all(jnp.broadcast_to(shard[None], (blocks, rows, 2 * depth)),...]
  transfers between devices with their start and end apart: 4 -> 9, of which waited for: 4 -> 7; matrix products, arithmetic and copies ran while one was open for 2% -> 10% of each run, Pallas kernels for 0% -> 0%
where the time goes in v1:
time: 267 us; the launch traced here: 266 us
  waiting for transfers between devices  124 us (46%)
  blocking collectives  47.7 us (18%)
  starting transfers between devices  31.5 us (12%)
  matrix products  20 us (7%)
  other arithmetic  16.8 us (6%)
  between operations  15.8 us (6%)
  local copies, waits for them, and re-layouts  9.15 us (3%)
    all_gather x1, waiting for transfers between devices, per_device(): trio = lax.all_gather(pair, ('zh', 'zl'), axis=0, tiled=True)  48.2 us
    all_to_all x1, blocking collectives, per_device(): lax.all_to_all(parts, ('zh', 'xh'), 0, 0, tiled=True).astype(jnp.float32)  47.7 us
    ppermute x6, waiting for transfers between devices, swap(): return lax.ppermute(x, axis, [(0, 1), (1, 0)])  37.9 us
    all_to_all x1, waiting for transfers between devices, per_device(): lax.all_to_all(jnp.broadcast_to(shard[None], (blocks, rows, 2 * depth)),...  28.6 us
    ppermute x6, starting transfers between devices, swap(): return lax.ppermute(x, axis, [(0, 1), (1, 0)])  16.1 us
    all_to_all x1, waiting for transfers between devices, per_device(): lax.all_to_all(in_part.astype(jnp.bfloat16).reshape(blocks, rows, depth),...  9.69 us
    dot_general x3, matrix products, contract_rows(): lax.dot_general(left, right, (((0,), (0,)), ((), ())), preferred_element_...  8.21 us
    all_to_all x1, starting transfers between devices, per_device(): lax.all_to_all(jnp.broadcast_to(shard[None], (blocks, rows, 2 * depth)),...  7.97 us
  transfers between devices with their start and end apart: 9, of which 7 were waited for; matrix products, arithmetic and copies ran while one was open for 10% of the time, Pallas kernels for 0%

profile of v1, /device:TPU:4, one launch (start us, length us, event | category | flops | bytes accessed | tf_op | source)
XLA Modules:
  0.0 265.5 jit_solution(10223095779749263783)
XLA Ops:
  9.1 8.0 %all-to-all-start = ((bf16[16,32,1024]{2,1,0:T(8,128)(2,1)}), bf16[16,32,1024]{2,1,0:T(8,128)(2,1)S(1)}, u32[]{:S(2)}, u32[]{:S(2)}) async-start(bf16[16,32,1024]{2,1,0:T(8,128)(2,1)} %broadcast_in_dim.12), calls=%async_computation | async-start | bytes 2097152 | tf_op jit(solution)/shard_map/all_to_all | solution.py:58
  17.1 28.6 %all-to-all-done = bf16[16,32,1024]{2,1,0:T(8,128)(2,1)S(1)} async-done(((bf16[16,32,1024]{2,1,0:T(8,128)(2,1)}), bf16[16,32,1024]{2,1,0:T(8,128)(2,1)S(1)}, u32[]{:S(2)}, u32[]{:S(2)}) %all-to-all-start) | async-done | bytes 1048608 | tf_op jit(solution)/shard_map/all_to_all | solution.py:58
  47.7 4.3 %collective-permute-start.1 = (bf16[2,128,1024]{2,1,0:T(8,128)(2,1)S(1)}, bf16[2,128,1024]{2,1,0:T(8,128)(2,1)}, u32[]{:S(2)}, u32[]{:S(2)}) collective-permute-start(bf16[2,128,1024]{2,1,0:T(8,128)(2,1)S(1)} %get-tuple-element.11), channel_id=1, source_target_pairs={{0,64},{64,0},{1,65},{65,1},{2,66},{66,2},{3,67},{67,3},{4,68},{68... | collective-permute-start | bytes 1572872 | tf_op jit(solution)/shard_map/ppermute | solution.py:38
  52.0 12.7 %collective-permute-done.1 = bf16[2,128,1024]{2,1,0:T(8,128)(2,1)} collective-permute-done((bf16[2,128,1024]{2,1,0:T(8,128)(2,1)S(1)}, bf16[2,128,1024]{2,1,0:T(8,128)(2,1)}, u32[]{:S(2)}, u32[]{:S(2)}) %collective-permute-start.1) | collective-permute-done | bytes 524320 | tf_op jit(solution)/shard_map/ppermute | solution.py:38
  67.9 3.6 %collective-permute-start.3 = (bf16[1536,512]{1,0:T(8,128)(2,1)}, bf16[1536,512]{1,0:T(8,128)(2,1)}, u32[]{:S(2)}, u32[]{:S(2)}) collective-permute-start(bf16[1536,512]{1,0:T(8,128)(2,1)} %pad_maximum_fusion), channel_id=1, source_target_pairs={{0,64},{64,0},{1,65},{65,1},{2,66},{66,2},{3,67},{67,3},{4,68},{68... | collective-permute-start | bytes 4718600 | tf_op jit(solution)/shard_map/ppermute | solution.py:38
  71.5 2.2 concatenate.50
  75.9 2.2 concatenate.51
  78.2 4.4 %maximum_maximum_fusion = bf16[512,2,2,512]{3,2,0,1:T(2,128)(2,1)S(1)} fusion(bf16[256,1,2,512]{3,2,0,1:T(2,128)(2,1)} %concatenate.51, bf16[256,1,2,512]{3,2,0,1:T(2,128)(2,1)} %concatenate.50, bf16[512,1,2,512]{3,2,0,1:T(2,128)(2,1)S(1)} %concatenate.49), kind=kLoop, calls=%fused_computation.2 | loop fusion | flops 2097152 | bytes 4194304 | tf_op jit(solution)/shard_map/concatenate | solution.py:82
  82.5 5.5 %fusion.1 = (bf16[]{:T(256)}, bf16[]{:T(256)}) fusion(bf16[512,2,2,512]{3,2,0,1:T(2,128)(2,1)S(1)} %maximum_maximum_fusion), kind=kLoop, calls=%fused_computation.6 | loop fusion | flops 2097150 | bytes 2097156 | tf_op jit(solution)/shard_map/reduce_max | solution.py:42
  91.1 15.8 %collective-permute-done.3 = bf16[1536,512]{1,0:T(8,128)(2,1)} collective-permute-done((bf16[1536,512]{1,0:T(8,128)(2,1)}, bf16[1536,512]{1,0:T(8,128)(2,1)}, u32[]{:S(2)}, u32[]{:S(2)}) %collective-permute-start.3) | collective-permute-done | bytes 1572896 | tf_op jit(solution)/shard_map/ppermute | solution.py:38
  106.9 2.4 fusion.6
  109.3 2.4 fusion.5
  113.5 2.5 concatenate.57
  116.0 47.7 %all_to_all.15 = f16[8,64,1664]{2,1,0:T(8,128)(2,1)S(1)} all-to-all(f16[8,64,1664]{2,1,0:T(8,128)(2,1)S(1)} %concatenate.57), channel_id=1, replica_groups=mesh['zh'=4,'zl'=2,'xh'=2,'y'=8,'xl'=2,'c'=2] {'zh','xh'}, dimensions={0} | all-to-all | bytes 3407872 | tf_op jit(solution)/shard_map/all_to_all | solution.py:98
  164.7 2.3 collective-permute-start.4
  167.0 6.8 %collective-permute-done.4 = bf16[64,1536]{1,0:T(8,128)(2,1)S(1)} collective-permute-done((bf16[64,1536]{1,0:T(8,128)(2,1)S(1)}, bf16[64,1536]{1,0:T(8,128)(2,1)S(1)}, u32[]{:S(2)}, u32[]{:S(2)}) %collective-permute-start.4) | collective-permute-done | bytes 196640 | tf_op jit(solution)/shard_map/ppermute | solution.py:38
  174.6 48.2 %all-gather.2.cloned.1.call-done = bf16[1024,1536]{1,0:T(8,128)(2,1)} async-done(((bf16[128,1536]{1,0:T(8,128)(2,1)}), bf16[1024,1536]{1,0:T(8,128)(2,1)}) %all-gather.2.cloned.1.call-update) | async-done | bytes 3145744 | tf_op jit(solution)/shard_map/all_gather | solution.py:110
  226.9 2.1 collective-permute-start.5
  229.0 2.6 collective-permute-done.5
  232.6 7.5 %all-to-all-start.2 = ((bf16[16,32,512]{2,1,0:T(8,128)(2,1)}), bf16[16,32,512]{2,1,0:T(8,128)(2,1)S(1)}, u32[]{:S(2)}, u32[]{:S(2)}) async-start(bf16[16,32,512]{2,1,0:T(8,128)(2,1)} %bitcast.13), calls=%async_computation.2 | async-start | bytes 1048576 | tf_op jit(solution)/shard_map/all_to_all | solution.py:116
  240.1 3.0 %convolution_convert_fusion = bf16[512,512]{1,0:T(8,128)(2,1)} fusion(bf16[512,1024]{1,0:T(8,128)(2,1)} %collective-permute-done, bf16[512,1024]{1,0:T(8,128)(2,1)S(1)} %bitcast.43, bf16[1024,1536]{1,0:T(8,128)(2,1)} %all-gather.2.cloned.1.call-done), kind=kOutput, calls=%fused_computation.20 | convolution fusion | flops 539230208 | bytes 3670016 | tf_op jit(solution)/shard_map/dot_general | solution.py:22
  243.1 2.6 convolution_convert_fusion.1
  245.7 2.6 convolution_convert_fusion.2
  248.3 9.7 %all-to-all-done.2 = bf16[16,32,512]{2,1,0:T(8,128)(2,1)S(1)} async-done(((bf16[16,32,512]{2,1,0:T(8,128)(2,1)}), bf16[16,32,512]{2,1,0:T(8,128)(2,1)S(1)}, u32[]{:S(2)}, u32[]{:S(2)}) %all-to-all-start.2) | async-done | bytes 524320 | tf_op jit(solution)/shard_map/all_to_all | solution.py:116
  (45 shorter events, 19.9 us)
Async XLA Ops:
  9.0 57.5 %copy-start = (bf16[512,512]{1,0:T(8,128)(2,1)S(1)}, bf16[512,512]{1,0:T(8,128)(2,1)}, u32[]{:S(2)}) copy-start(bf16[512,512]{1,0:T(8,128)(2,1)} %param.7) | copy-start | bytes 1572868
  9.0 57.6 %copy-start.1 = (bf16[512,512]{1,0:T(8,128)(2,1)S(1)}, bf16[512,512]{1,0:T(8,128)(2,1)}, u32[]{:S(2)}) copy-start(bf16[512,512]{1,0:T(8,128)(2,1)} %param.8) | copy-start | bytes 1572868
  9.1 57.6 %copy-start.4 = (bf16[512,512]{1,0:T(8,128)(2,1)S(1)}, bf16[512,512]{1,0:T(8,128)(2,1)}, u32[]{:S(2)}) copy-start(bf16[512,512]{1,0:T(8,128)(2,1)} %param.9) | copy-start | bytes 1572868
  9.1 36.7 %all-to-all-start = ((bf16[16,32,1024]{2,1,0:T(8,128)(2,1)}), bf16[16,32,1024]{2,1,0:T(8,128)(2,1)S(1)}, u32[]{:S(2)}, u32[]{:S(2)}) async-start(bf16[16,32,1024]{2,1,0:T(8,128)(2,1)} %broadcast_in_dim.12), calls=%async_computation | async-start | bytes 2097152 | tf_op jit(solution)/shard_map/all_to_all | solution.py:58
  17.0 205.8 %all-gather.2.cloned.1.call-start = ((), (), s32[]{:S(2)}) async-start(), calls=%async_computation.3 | async-start | bytes 3538944 | tf_op jit(solution)/shard_map/all_gather | solution.py:110
  45.7 22.2 %copy-start.2 = (bf16[16,32,1024]{2,1,0:T(8,128)(2,1)}, bf16[16,32,1024]{2,1,0:T(8,128)(2,1)S(1)}, u32[]{:S(2)}) copy-start(bf16[16,32,1024]{2,1,0:T(8,128)(2,1)S(1)} %all-to-all-done) | copy-start | bytes 3145732
  45.7 28.0 %collective-permute-start = (bf16[512,1024]{1,0:T(8,128)(2,1)S(1)}, bf16[512,1024]{1,0:T(8,128)(2,1)}, u32[]{:S(2)}, u32[]{:S(2)}) collective-permute-start(bf16[512,1024]{1,0:T(8,128)(2,1)S(1)} %bitcast.41), channel_id=1, source_target_pairs={{0,1},{1,0},{2,3},{3,2},{4,5},{5,4},{6,7},{7,6},{8,9},{9,8},{10,11... | collective-permute-start | bytes 3145736 | tf_op jit(solution)/shard_map/ppermute | solution.py:38
  47.7 17.0 %collective-permute-start.1 = (bf16[2,128,1024]{2,1,0:T(8,128)(2,1)S(1)}, bf16[2,128,1024]{2,1,0:T(8,128)(2,1)}, u32[]{:S(2)}, u32[]{:S(2)}) collective-permute-start(bf16[2,128,1024]{2,1,0:T(8,128)(2,1)S(1)} %get-tuple-element.11), channel_id=1, source_target_pairs={{0,64},{64,0},{1,65},{65,1},{2,66},{66,2},{3,67},{67,3},{4,68},{68... | collective-permute-start | bytes 1572872 | tf_op jit(solution)/shard_map/ppermute | solution.py:38
  64.7 11.2 %collective-permute-start.2 = (bf16[256,1024]{1,0:T(8,128)(2,1)}, bf16[256,1024]{1,0:T(8,128)(2,1)}, u32[]{:S(2)}, u32[]{:S(2)}) collective-permute-start(bf16[256,1024]{1,0:T(8,128)(2,1)} %bitcast.9), channel_id=1, source_target_pairs={{0,1},{1,0},{2,3},{3,2},{4,5},{5,4},{6,7},{7,6},{8,9},{9,8},{10,11... | collective-permute-start | bytes 1572872 | tf_op jit(solution)/shard_map/ppermute | solution.py:38
  67.9 39.0 %collective-permute-start.3 = (bf16[1536,512]{1,0:T(8,128)(2,1)}, bf16[1536,512]{1,0:T(8,128)(2,1)}, u32[]{:S(2)}, u32[]{:S(2)}) collective-permute-start(bf16[1536,512]{1,0:T(8,128)(2,1)} %pad_maximum_fusion), channel_id=1, source_target_pairs={{0,64},{64,0},{1,65},{65,1},{2,66},{66,2},{3,67},{67,3},{4,68},{68... | collective-permute-start | bytes 4718600 | tf_op jit(solution)/shard_map/ppermute | solution.py:38
  89.5 1.0 copy-start.5
  164.7 9.1 %collective-permute-start.4 = (bf16[64,1536]{1,0:T(8,128)(2,1)S(1)}, bf16[64,1536]{1,0:T(8,128)(2,1)S(1)}, u32[]{:S(2)}, u32[]{:S(2)}) collective-permute-start(bf16[64,1536]{1,0:T(8,128)(2,1)S(1)} %pad_maximum_fusion.7), channel_id=1, source_target_pairs={{0,32},{32,0},{1,33},{33,1},{2,34},{34,2},{3,35},{35,3},{4,36},{36... | collective-permute-start | bytes 589832 | tf_op jit(solution)/shard_map/ppermute | solution.py:38
  226.9 13.2 %copy-start.3 = (bf16[16,32,1024]{2,1,0:T(8,128)(2,1)S(1)}, bf16[16,32,1024]{2,1,0:T(8,128)(2,1)}, u32[]{:S(2)}) copy-start(bf16[16,32,1024]{2,1,0:T(8,128)(2,1)} %copy-done.2) | copy-start | bytes 3145732
  226.9 4.7 %collective-permute-start.5 = (f32[512,512]{1,0:T(8,128)S(1)}, f32[512,512]{1,0:T(8,128)S(1)}, u32[]{:S(2)}, u32[]{:S(2)}) collective-permute-start(f32[512,512]{1,0:T(8,128)S(1)} %slice.125), channel_id=1, source_target_pairs={{0,1},{1,0},{2,3},{3,2},{4,5},{5,4},{6,7},{7,6},{8,9},{9,8},{10,11... | collective-permute-start | bytes 3145736 | tf_op jit(solution)/shard_map/ppermute | solution.py:38
  232.6 25.4 %all-to-all-start.2 = ((bf16[16,32,512]{2,1,0:T(8,128)(2,1)}), bf16[16,32,512]{2,1,0:T(8,128)(2,1)S(1)}, u32[]{:S(2)}, u32[]{:S(2)}) async-start(bf16[16,32,512]{2,1,0:T(8,128)(2,1)} %bitcast.13), calls=%async_computation.2 | async-start | bytes 1048576 | tf_op jit(solution)/shard_map/all_to_all | solution.py:116
  240.1 3.1 %copy-start.6 = (bf16[1024,1536]{1,0:T(8,128)(2,1)S(1)}, bf16[1024,1536]{1,0:T(8,128)(2,1)}, u32[]{:S(2)}) copy-start(bf16[1024,1536]{1,0:T(8,128)(2,1)} %all-gather.2.cloned.1.call-done) | copy-start | bytes 9437188
Sparse Core Ops, SparseCore 0:
  174.7 48.0 all-gather.1

commit v2 on v0

v2 whole, which is shorter than its diff:
```python
import functools

import jax
import jax.numpy as jnp
from jax import lax
from jax.experimental import pallas as pl
from jax.experimental.pallas import tpu as pltpu
from jax.sharding import Mesh, PartitionSpec as P

ROW = ("zh", "zl", "xh")
COL = ("y", "xl", "c")
LANES = 128
TAIL = 16


def swiglu_back(gate, up, hidden_grad):
    sig = jax.nn.sigmoid(gate)
    act = gate * sig
    hidden = (act * up).astype(jnp.bfloat16)
    gate_grad = (hidden_grad * up * sig * (1.0 + gate * (1.0 - sig))).astype(jnp.bfloat16)
    up_grad = (hidden_grad * act).astype(jnp.bfloat16)
    return (hidden, gate_grad, up_grad)


def contract_rows(left, right):
    return lax.dot_general(
        left, right, (((0,), (0,)), ((), ())), preferred_element_type=jnp.float32
    )


def contract_cols(left, right):
    return lax.dot_general(
        left, right, (((1,), (1,)), ((), ())), preferred_element_type=jnp.float32
    )


def matmul(left, right):
    return jnp.dot(left, right, preferred_element_type=jnp.float32)


def swap(x, axis):
    return lax.ppermute(x, axis, [(0, 1), (1, 0)])


def forward_kernel(half_ref, own, other, ext, ext_other, gate_w, up_w, down_w, far, out):
    half = half_ref[0]
    depth = gate_w.shape[0]
    near = [source[i, half] for source in (own, other) for i in range(own.shape[0])]
    near = jnp.concatenate(near, axis=0)
    beyond = jnp.concatenate([ext[...], ext_other[...]], axis=0)
    group, rows = out.shape[0], near.shape[0] // out.shape[0]
    lane_blocks = gate_w.shape[1] // LANES
    place = lax.broadcasted_iota(jnp.int32, (TAIL, LANES), 0)
    tail = jnp.zeros((TAIL, LANES), jnp.float32)
    for n in range(3):
        far_w = far[n * depth : (n + 1) * depth, :]
        if n == 2:
            part = contract_cols(near[:, depth:], down_w[...]) + contract_cols(
                beyond[:, depth:], far_w
            )
        else:
            near_w = (gate_w, up_w)[n][...]
            part = matmul(near[:, :depth], near_w) + matmul(beyond[:, :depth], far_w)
        top = jnp.max(jnp.abs(part), axis=0, keepdims=True)
        top = jnp.max(top, axis=1, keepdims=True)
        exponent = jnp.floor(14.0 - jnp.log2(jnp.maximum(top, 1e-30)))
        exponent = jnp.clip(exponent, -100.0, 100.0)
        part = part * jnp.exp2(exponent)
        for j in range(group):
            for q in range(lane_blocks):
                at = (n * lane_blocks + q) * rows
                out[j, at : at + rows, :] = part[
                    j * rows : (j + 1) * rows, q * LANES : (q + 1) * LANES
                ]
        tail = jnp.where(place == n, exponent, tail)
    for j in range(group):
        out[j, 3 * lane_blocks * rows :, :] = tail


def middle_kernel(parts, trio):
    rows, ff = trio.shape[0], trio.shape[1] // 3
    lane_blocks = ff // LANES
    tail = 3 * lane_blocks * rows
    scales = [jnp.exp2(-parts[:, tail + n : tail + n + 1, :]) for n in range(3)]
    for q in range(lane_blocks):
        sums = []
        for n in range(3):
            at = (n * lane_blocks + q) * rows
            sums.append(jnp.sum(parts[:, at : at + rows, :] * scales[n], axis=0))
        for n, value in enumerate(swiglu_back(*sums)):
            at = n * ff + q * LANES
            trio[:, at : at + LANES] = value


def backward_kernel(zh_size, place, gate_w, up_w, trio_in, *refs):
    size = 2 * zh_size
    rights, refs = refs[:zh_size], refs[zh_size:]
    lefts, refs = refs[: zh_size - 1], refs[zh_size - 1 :]
    beside, (trio, in_own, in_other) = refs[: zh_size + 1], refs[zh_size + 1 :]
    rows, ff = trio_in.shape[0], gate_w.shape[1]
    z, xh = place[0], place[1]

    def put(distance, mine, others):
        at = 2 * rows * lax.rem(z + distance + size, size)
        trio[pl.ds(pl.multiple_of(at + rows * xh, rows), rows), :] = mine
        trio[pl.ds(pl.multiple_of(at + rows * (1 - xh), rows), rows), :] = others

    put(0, trio_in[...], beside[0][...])
    for k in range(1, zh_size):
        put(-k, rights[k - 1][...], beside[k][:rows, :])
        put(k, lefts[k - 1][...], beside[k][rows:, :])
    put(-zh_size, rights[-1][...], beside[-1][...])
    share = in_own.shape[0]
    for part, target in ((1, in_other), (0, in_own)):
        at = slice(part * share, (part + 1) * share)
        target[...] = contract_cols(trio[at, ff : 2 * ff], gate_w[...]) + contract_cols(
            trio[at, 2 * ff :], up_w[...]
        )


def early(x):
    return pl.pallas_call(
        lambda x_ref, out_ref: None,
        out_shape=jax.ShapeDtypeStruct(x.shape, x.dtype),
        in_specs=[pl.BlockSpec(memory_space=pltpu.HBM)],
        out_specs=pl.BlockSpec(memory_space=pltpu.HBM),
        input_output_aliases={0: 0},
        cost_estimate=pl.CostEstimate(flops=10**11, bytes_accessed=0, transcendentals=0),
        name="exchanged",
    )(x)


def turn(x, size, step):
    return lax.ppermute(x, ("zh", "zl"), [(i, (i + step) % size) for i in range(size)])


def pick(first, x):
    return jnp.where(first, x[:, 0], x[:, 1])


def per_device(zh_size, blocks, tokens, out_grad, gate_weight, up_weight, down_weight):
    zl = lax.axis_index("zl")
    xh = lax.axis_index("xh")
    first = zl == 0
    rows, depth = tokens.shape
    ff = gate_weight.shape[1]
    group = 2 * zh_size

    far = swap(jnp.concatenate([gate_weight, up_weight, down_weight], axis=0), "zl")

    shard = jnp.concatenate([tokens, out_grad], axis=1)
    own = lax.all_to_all(
        jnp.broadcast_to(shard[None], (blocks, rows, 2 * depth)), ("y", "xl"), 0, 0, tiled=True
    )
    own, far = lax.optimization_barrier((own, early(far)))
    own = own.reshape(zh_size // 2, 2, -1, 2 * depth)
    ext = swap(pick(~first, own), "zl").reshape(-1, 2 * depth)
    other = swap(own, "c")
    ext_other = swap(ext, "c")

    half_tokens = own.size // (2 * depth)
    token_rows = half_tokens // group
    sent_rows = 3 * (ff // LANES) * token_rows
    parts = pl.pallas_call(
        forward_kernel,
        out_shape=jax.ShapeDtypeStruct((group, sent_rows + TAIL, LANES), jnp.float32),
        in_specs=[pl.BlockSpec(memory_space=pltpu.SMEM)]
        + [pl.BlockSpec(memory_space=pltpu.VMEM)] * 8,
        out_specs=pl.BlockSpec(memory_space=pltpu.VMEM),
        compiler_params=pltpu.CompilerParams(vmem_limit_bytes=40 * 2**20),
        cost_estimate=pl.CostEstimate(
            flops=12 * half_tokens * depth * ff,
            bytes_accessed=9 * 2**20,
            transcendentals=0,
        ),
        name="forward_sums",
    )(
        zl.astype(jnp.int32)[None], own, other, ext, ext_other,
        gate_weight, up_weight, down_weight, far,
    )
    parts = lax.all_to_all(parts.astype(jnp.float16), ("zh", "xh"), 0, 0, tiled=True)
    trio = pl.pallas_call(
        middle_kernel,
        out_shape=jax.ShapeDtypeStruct((token_rows, 3 * ff), jnp.bfloat16),
        in_specs=[pl.BlockSpec(memory_space=pltpu.VMEM)],
        out_specs=pl.BlockSpec(memory_space=pltpu.VMEM),
        compiler_params=pltpu.CompilerParams(vmem_limit_bytes=24 * 2**20),
        cost_estimate=pl.CostEstimate(
            flops=8 * group * token_rows * ff,
            bytes_accessed=4 * 2**20,
            transcendentals=token_rows * ff,
        ),
        name="hidden_and_grads",
    )(parts.astype(jnp.float32))

    right, left = [trio], [trio]
    beside = [swap(trio, "xh")]
    for step in range(1, zh_size):
        right.append(turn(right[-1], 2 * zh_size, 1))
        left.append(turn(left[-1], 2 * zh_size, -1))
        if step >= 2:
            right[-1], left[-1], beside[step - 2] = lax.optimization_barrier(
                (right[-1], left[-1], beside[step - 2])
            )
        beside.append(swap(jnp.concatenate([right[-1], left[-1]], axis=0), "xh"))
    right.append(turn(right[-1], 2 * zh_size, 1))
    beside.append(swap(right[-1], "xh"))

    place = jnp.stack([2 * lax.axis_index("zh") + zl, xh]).astype(jnp.int32)
    blocks_in = [trio] + right[1:] + left[1:] + beside
    share = half_tokens
    trio, in_own, in_other = pl.pallas_call(
        functools.partial(backward_kernel, zh_size),
        out_shape=(
            jax.ShapeDtypeStruct((2 * share, 3 * ff), jnp.bfloat16),
            jax.ShapeDtypeStruct((share, depth), jnp.float32),
            jax.ShapeDtypeStruct((share, depth), jnp.float32),
        ),
        in_specs=[pl.BlockSpec(memory_space=pltpu.SMEM)]
        + [pl.BlockSpec(memory_space=pltpu.VMEM)] * (2 + len(blocks_in)),
        out_specs=[pl.BlockSpec(memory_space=pltpu.VMEM)] * 3,
        compiler_params=pltpu.CompilerParams(vmem_limit_bytes=40 * 2**20),
        cost_estimate=pl.CostEstimate(
            flops=8 * share * depth * ff, bytes_accessed=9 * 2**20, transcendentals=0
        ),
        name="input_gradient",
    )(place, gate_weight, up_weight, *blocks_in)
    hidden, gate_grad, up_grad = trio[:, :ff], trio[:, ff : 2 * ff], trio[:, 2 * ff :]

    every = jnp.concatenate([x.reshape(-1, 2 * depth) for x in (own, other)], axis=0)
    inputs, grads = every[:, :depth], every[:, depth:]
    in_part = in_own + swap(in_other, "c")
    in_part = lax.all_to_all(
        in_part.astype(jnp.bfloat16).reshape(blocks, rows, depth), ("y", "xl"), 0, 0, tiled=True
    )
    in_grad = jnp.sum(in_part.astype(jnp.float32), axis=0).astype(jnp.bfloat16)

    down_wgrad = contract_rows(hidden, grads).astype(jnp.bfloat16)
    gate_wgrad = contract_rows(inputs, gate_grad).astype(jnp.bfloat16)
    up_wgrad = contract_rows(inputs, up_grad).astype(jnp.bfloat16)
    return (in_grad, gate_wgrad, up_wgrad, down_wgrad)


def solution(mesh):
    row, col = mesh.devices.shape
    zh_size, y_size = row // 4, col // 4
    fine = Mesh(
        mesh.devices.reshape(zh_size, 2, 2, y_size, 2, 2), ("zh", "zl", "xh", "y", "xl", "c")
    )

    def body(*args):
        return per_device(zh_size, 2 * y_size, *args)

    in_specs = (P(COL, ROW), P(COL, ROW), P(ROW, COL), P(ROW, COL), P(COL, ROW))
    out_specs = (P(COL, ROW), P(ROW, COL), P(ROW, COL), P(COL, ROW))
    return jax.shard_map(
        body, mesh=fine, in_specs=in_specs, out_specs=out_specs, check_vma=False
    )
```

time: 586 us -> 213 us (0.36)
  waiting for transfers between devices: 546 us -> 65.8 us
  starting transfers between devices: 0.16 us -> 68.4 us
  blocking collectives: 0 us -> 52.4 us
  between operations: 13.8 us -> 1.04 us
  matrix products: 18.1 us -> 5.97 us
  Pallas kernels: 0 us -> 6.82 us
    psum x1 -> x0, waiting for transfers between devices: 293 us -> none  [per_device(): gate, up, hidden_grad = lax.psum((gate_part, up_part, hidden_part), 'row')]
    all_gather x2 -> x0, waiting for transfers between devices: 135 us -> none  [the longest x1 72 us: per_device(): inputs = lax.all_gather(tokens, 'col', axis=0, tiled=True)]
    reduce_scatter x1 -> x0, waiting for transfers between devices: 117 us -> none  [per_device(): lax.psum_scatter(contract_cols(gate_grad, gate_weight) + contract_cols(up...]
    ppermute x0 -> x17, starting transfers between devices: none -> 52.8 us  [the longest x10 30.9 us: swap(): return lax.ppermute(x, axis, [(0, 1), (1, 0)])]
    all_to_all x0 -> x1, blocking collectives: none -> 52.4 us  [per_device(): lax.all_to_all(parts.astype(jnp.float16), ('zh', 'xh'), 0, 0, tiled=True)]
    ppermute x0 -> x17, waiting for transfers between devices: none -> 51.5 us  [the longest x10 46.5 us: swap(): return lax.ppermute(x, axis, [(0, 1), (1, 0)])]
    all_to_all x0 -> x2, starting transfers between devices: none -> 15.7 us  [the longest x1 7.84 us: per_device(): lax.all_to_all(in_part.astype(jnp.bfloat16).reshape(blocks, rows, depth),...]
    all_to_all x0 -> x2, waiting for transfers between devices: none -> 14.3 us  [the longest x1 11.9 us: per_device(): lax.all_to_all(in_part.astype(jnp.bfloat16).reshape(blocks, rows, depth),...]
  transfers between devices with their start and end apart: 4 -> 19, of which waited for: 4 -> 9; matrix products, arithmetic and copies ran while one was open for 2% -> 4% of each run, Pallas kernels for 0% -> 0%
where the time goes in v2:
time: 213 us; the launch traced here: 212 us
  starting transfers between devices  68.4 us (32%)
  waiting for transfers between devices  65.8 us (31%)
  blocking collectives  52.4 us (25%)
  Pallas kernels  6.82 us (3%)
  other arithmetic  6.4 us (3%)
  matrix products  5.97 us (3%)
  local copies, waits for them, and re-layouts  5.36 us (3%)
    all_to_all x1, blocking collectives, per_device(): lax.all_to_all(parts.astype(jnp.float16), ('zh', 'xh'), 0, 0, tiled=True)  52.4 us
    ppermute x10, waiting for transfers between devices, swap(): return lax.ppermute(x, axis, [(0, 1), (1, 0)])  46.5 us
    ppermute x10, starting transfers between devices, swap(): return lax.ppermute(x, axis, [(0, 1), (1, 0)])  30.9 us
    ppermute x7, starting transfers between devices, turn(): lax.ppermute(x, ('zh', 'zl'), [(i, (i + step) % size) for i in range(size)])  21.9 us
    all_to_all x1, waiting for transfers between devices, per_device(): lax.all_to_all(in_part.astype(jnp.bfloat16).reshape(blocks, rows, depth),...  11.9 us
    all_to_all x1, starting transfers between devices, per_device(): lax.all_to_all(in_part.astype(jnp.bfloat16).reshape(blocks, rows, depth),...  7.84 us
    all_to_all x1, starting transfers between devices, per_device(): lax.all_to_all(jnp.broadcast_to(shard[None], (blocks, rows, 2 * depth)),...  7.84 us
    dot_general x3, matrix products, contract_rows(): lax.dot_general(left, right, (((0,), (0,)), ((), ())), preferred_element_...  5.97 us
  transfers between devices with their start and end apart: 19, of which 9 were waited for; matrix products, arithmetic and copies ran while one was open for 4% of the time, Pallas kernels for 0%

profile of v2, /device:TPU:4, one launch (start us, length us, event | category | flops | bytes accessed | tf_op | source)
XLA Modules:
  0.0 212.2 jit_solution(14521374480556363492)
XLA Ops:
  0.7 2.6 %pad_maximum_fusion = bf16[1536,512]{1,0:T(8,128)(2,1)} fusion(bf16[512,512]{1,0:T(8,128)(2,1)} %down_w.1, bf16[512,512]{1,0:T(8,128)(2,1)} %up_w.3, bf16[512,512]{1,0:T(8,128)(2,1)} %gate_w.3), kind=kLoop, calls=%fused_computation.2 | loop fusion | flops 4718592 | bytes 3145728 | tf_op jit(solution)/shard_map/concatenate | solution.py:149
  3.3 4.3 %collective-permute-start = (bf16[1536,512]{1,0:T(8,128)(2,1)}, bf16[1536,512]{1,0:T(8,128)(2,1)}, u32[]{:S(2)}, u32[]{:S(2)}) collective-permute-start(bf16[1536,512]{1,0:T(8,128)(2,1)} %pad_maximum_fusion), channel_id=1, source_target_pairs={{0,64},{64,0},{1,65},{65,1},{2,66},{66,2},{3,67},{67,3},{4,68},{68... | collective-permute-start | bytes 4718600 | tf_op jit(solution)/shard_map/ppermute | solution.py:42
  8.7 7.8 %all-to-all-start = ((bf16[16,32,1024]{2,1,0:T(8,128)(2,1)}), bf16[16,32,1024]{2,1,0:T(8,128)(2,1)S(1)}, u32[]{:S(2)}, u32[]{:S(2)}) async-start(bf16[16,32,1024]{2,1,0:T(8,128)(2,1)} %broadcast_in_dim.10), calls=%async_computation | async-start | bytes 2097152 | tf_op jit(solution)/shard_map/all_to_all | solution.py:152
  16.6 25.7 %collective-permute-done.x_ref = bf16[1536,512]{1,0:T(8,128)(2,1)} collective-permute-done((bf16[1536,512]{1,0:T(8,128)(2,1)}, bf16[1536,512]{1,0:T(8,128)(2,1)}, u32[]{:S(2)}, u32[]{:S(2)}) %collective-permute-start) | collective-permute-done | bytes 1572896 | tf_op jit(solution)/shard_map/ppermute | solution.py:42
  44.6 2.5 %collective-permute-start.2 = (bf16[2,128,1024]{2,1,0:T(8,128)(2,1)S(1)}, bf16[2,128,1024]{2,1,0:T(8,128)(2,1)S(1)}, u32[]{:S(2)}, u32[]{:S(2)}) collective-permute-start(bf16[2,128,1024]{2,1,0:T(8,128)(2,1)S(1)} %fusion.5), channel_id=1, source_target_pairs={{0,64},{64,0},{1,65},{65,1},{2,66},{66,2},{3,67},{67,3},{4,68},{68... | collective-permute-start | bytes 1572872 | tf_op jit(solution)/shard_map/ppermute | solution.py:42
  49.1 8.2 %collective-permute-done.2 = bf16[2,128,1024]{2,1,0:T(8,128)(2,1)S(1)} collective-permute-done((bf16[2,128,1024]{2,1,0:T(8,128)(2,1)S(1)}, bf16[2,128,1024]{2,1,0:T(8,128)(2,1)S(1)}, u32[]{:S(2)}, u32[]{:S(2)}) %collective-permute-start.2) | collective-permute-done | bytes 524320 | tf_op jit(solution)/shard_map/ppermute | solution.py:42
  61.1 3.8 %forward_sums.1 = f32[8,784,128]{2,1,0:T(8,128)S(1)} custom-call(s32[1]{0:T(128)} %bitcast.2.half_ref, bf16[2,2,128,1024]{3,2,1,0:T(8,128)(2,1)S(1)} %bitcast.12, bf16[2,2,128,1024]{3,2,1,0:T(8,128)(2,1)S(1)} %collective-permute-done.1.other, bf16[256,1024]{1,0:T(8,128)(2,1)S(1)} %bitcast.20, bf16[256,1024]{1,0:T(8,128)(2,1)S(1)} %collective-permute-done.3.ext_other, ...), custom_call_target="tpu_custom_call" | custom-call | flops 1610612736 | bytes 9437184 | tf_op jit(solution)/shard_map/forward_sums/pallas_call | solution.py:164
  65.2 52.4 %all_to_all.15 = f16[8,784,128]{2,1,0:T(8,128)(2,1)S(1)} all-to-all(f16[8,784,128]{2,1,0:T(8,128)(2,1)S(1)} %convert_element_type.20), channel_id=1, replica_groups=mesh['zh'=4,'zl'=2,'xh'=2,'y'=8,'xl'=2,'c'=2] {'zh','xh'}, dimensions={0} | all-to-all | bytes 3211264 | tf_op jit(solution)/shard_map/all_to_all | solution.py:181
  118.1 2.6 %collective-permute-start.6 = (bf16[64,1536]{1,0:T(8,128)(2,1)S(1)}, bf16[64,1536]{1,0:T(8,128)(2,1)S(1)}, u32[]{:S(2)}, u32[]{:S(2)}) collective-permute-start(bf16[64,1536]{1,0:T(8,128)(2,1)S(1)} %hidden_and_grads.1.trio_in), channel_id=1, source_target_pairs={{0,448},{64,0},{128,64},{192,128},{256,192},{320,256},{384,320},{4... | collective-permute-start | bytes 589832 | tf_op jit(solution)/shard_map/ppermute | solution.py:134
  120.7 3.3 %collective-permute-start.4 = (bf16[64,1536]{1,0:T(8,128)(2,1)S(1)}, bf16[64,1536]{1,0:T(8,128)(2,1)S(1)}, u32[]{:S(2)}, u32[]{:S(2)}) collective-permute-start(bf16[64,1536]{1,0:T(8,128)(2,1)S(1)} %hidden_and_grads.1.trio_in), channel_id=1, source_target_pairs={{0,64},{64,128},{128,192},{192,256},{256,320},{320,384},{384,448},... | collective-permute-start | bytes 589832 | tf_op jit(solution)/shard_map/ppermute | solution.py:134
  123.9 3.6 %collective-permute-start.8 = (bf16[64,1536]{1,0:T(8,128)(2,1)S(1)}, bf16[64,1536]{1,0:T(8,128)(2,1)S(1)}, u32[]{:S(2)}, u32[]{:S(2)}) collective-permute-start(bf16[64,1536]{1,0:T(8,128)(2,1)S(1)} %hidden_and_grads.1.trio_in), channel_id=1, source_target_pairs={{0,32},{32,0},{1,33},{33,1},{2,34},{34,2},{3,35},{35,3},{4,36},{36... | collective-permute-start | bytes 589832 | tf_op jit(solution)/shard_map/ppermute | solution.py:42
  127.5 5.1 %collective-permute-start.7 = (bf16[64,1536]{1,0:T(8,128)(2,1)S(1)}, bf16[64,1536]{1,0:T(8,128)(2,1)S(1)}, u32[]{:S(2)}, u32[]{:S(2)}) collective-permute-start(bf16[64,1536]{1,0:T(8,128)(2,1)S(1)} %collective-permute-done.6.refs_4_), channel_id=1, source_target_pairs={{0,448},{64,0},{128,64},{192,128},{256,192},{320,256},{384,320},{4... | collective-permute-start | bytes 589832 | tf_op jit(solution)/shard_map/ppermute | solution.py:134
  134.6 2.8 %collective-permute-start.11 = (bf16[128,1536]{1,0:T(8,128)(2,1)S(1)}, bf16[128,1536]{1,0:T(8,128)(2,1)S(1)}, u32[]{:S(2)}, u32[]{:S(2)}) collective-permute-start(bf16[128,1536]{1,0:T(8,128)(2,1)S(1)} %pad_maximum_fusion.3), channel_id=1, source_target_pairs={{0,32},{32,0},{1,33},{33,1},{2,34},{34,2},{3,35},{35,3},{4,36},{36... | collective-permute-start | bytes 1179656 | tf_op jit(solution)/shard_map/ppermute | solution.py:42
  138.2 3.3 %collective-permute-done.5.refs_1_ = bf16[64,1536]{1,0:T(8,128)(2,1)S(1)} collective-permute-done((bf16[64,1536]{1,0:T(8,128)(2,1)S(1)}, bf16[64,1536]{1,0:T(8,128)(2,1)S(1)}, u32[]{:S(2)}, u32[]{:S(2)}) %collective-permute-start.5) | collective-permute-done | bytes 196640 | tf_op jit(solution)/shard_map/ppermute | solution.py:134
  143.4 5.1 %collective-permute-start.10 = (bf16[64,1536]{1,0:T(8,128)(2,1)S(1)}, bf16[64,1536]{1,0:T(8,128)(2,1)S(1)}, u32[]{:S(2)}, u32[]{:S(2)}) collective-permute-start(bf16[64,1536]{1,0:T(8,128)(2,1)S(1)} %collective-permute-done.7.refs_5_), channel_id=1, source_target_pairs={{0,448},{64,0},{128,64},{192,128},{256,192},{320,256},{384,320},{4... | collective-permute-start | bytes 589832 | tf_op jit(solution)/shard_map/ppermute | solution.py:134
  149.3 2.8 %collective-permute-start.13 = (bf16[128,1536]{1,0:T(8,128)(2,1)}, bf16[128,1536]{1,0:T(8,128)(2,1)}, u32[]{:S(2)}, u32[]{:S(2)}) collective-permute-start(bf16[128,1536]{1,0:T(8,128)(2,1)} %pad_maximum_fusion.4), channel_id=1, source_target_pairs={{0,32},{32,0},{1,33},{33,1},{2,34},{34,2},{3,35},{35,3},{4,36},{36... | collective-permute-start | bytes 1179656 | tf_op jit(solution)/shard_map/ppermute | solution.py:42
  154.9 4.5 %collective-permute-start.14 = (bf16[128,1536]{1,0:T(8,128)(2,1)}, bf16[128,1536]{1,0:T(8,128)(2,1)}, u32[]{:S(2)}, u32[]{:S(2)}) collective-permute-start(bf16[128,1536]{1,0:T(8,128)(2,1)} %pad_maximum_fusion.5), channel_id=1, source_target_pairs={{0,32},{32,0},{1,33},{33,1},{2,34},{34,2},{3,35},{35,3},{4,36},{36... | collective-permute-start | bytes 1179656 | tf_op jit(solution)/shard_map/ppermute | solution.py:42
  161.1 4.5 %collective-permute-start.15 = (bf16[64,1536]{1,0:T(8,128)(2,1)}, bf16[64,1536]{1,0:T(8,128)(2,1)}, u32[]{:S(2)}, u32[]{:S(2)}) collective-permute-start(bf16[64,1536]{1,0:T(8,128)(2,1)} %collective-permute-done.12.refs_3_), channel_id=1, source_target_pairs={{0,32},{32,0},{1,33},{33,1},{2,34},{34,2},{3,35},{35,3},{4,36},{36... | collective-permute-start | bytes 589832 | tf_op jit(solution)/shard_map/ppermute | solution.py:42
  165.7 8.2 %collective-permute-done.15.refs_11_ = bf16[64,1536]{1,0:T(8,128)(2,1)} collective-permute-done((bf16[64,1536]{1,0:T(8,128)(2,1)}, bf16[64,1536]{1,0:T(8,128)(2,1)}, u32[]{:S(2)}, u32[]{:S(2)}) %collective-permute-start.15) | collective-permute-done | bytes 196640 | tf_op jit(solution)/shard_map/ppermute | solution.py:42
  175.8 2.7 %input_gradient.1 = (bf16[1024,1536]{1,0:T(8,128)(2,1)S(1)}, f32[512,512]{1,0:T(8,128)S(1)}, f32[512,512]{1,0:T(8,128)S(1)}) custom-call(s32[2]{0:T(128)S(1)} %pad_add_fusion.place, bf16[512,512]{1,0:T(8,128)(2,1)S(1)} %copy-done, bf16[512,512]{1,0:T(8,128)(2,1)S(1)} %copy-done.1, bf16[64,1536]{1,0:T(8,128)(2,1)S(1)} %hidden_and_grads.1.trio_in, ...), custom_call_target="tpu_custom_call" | custom-call | flops 1073741824 | bytes 9437184 | tf_op jit(solution)/shard_map/input_gradient/pallas_call | solution.py:212
  182.2 2.6 %collective-permute-done.16 = f32[512,512]{1,0:T(8,128)S(1)} collective-permute-done((f32[512,512]{1,0:T(8,128)S(1)}, f32[512,512]{1,0:T(8,128)S(1)}, u32[]{:S(2)}, u32[]{:S(2)}) %collective-permute-start.16) | collective-permute-done | bytes 1048608 | tf_op jit(solution)/shard_map/ppermute | solution.py:42
  185.7 7.8 %all-to-all-start.2 = ((bf16[16,32,512]{2,1,0:T(8,128)(2,1)}), bf16[16,32,512]{2,1,0:T(8,128)(2,1)S(1)}, u32[]{:S(2)}, u32[]{:S(2)}) async-start(bf16[16,32,512]{2,1,0:T(8,128)(2,1)} %bitcast.6), calls=%async_computation.2 | async-start | bytes 1048576 | tf_op jit(solution)/shard_map/all_to_all | solution.py:233
  193.6 2.9 %convolution_convert_fusion = bf16[512,512]{1,0:T(8,128)(2,1)} fusion(bf16[512,1024]{1,0:T(8,128)(2,1)S(1)} %bitcast.16, bf16[512,1024]{1,0:T(8,128)(2,1)S(1)} %bitcast.13, bf16[1024,1536]{1,0:T(8,128)(2,1)} %copy-done.9), kind=kOutput, calls=%fused_computation.3 | convolution fusion | flops 539230208 | bytes 3670016 | tf_op jit(solution)/shard_map/dot_general | solution.py:26
  199.6 11.9 %all-to-all-done.2 = bf16[16,32,512]{2,1,0:T(8,128)(2,1)S(1)} async-done(((bf16[16,32,512]{2,1,0:T(8,128)(2,1)}), bf16[16,32,512]{2,1,0:T(8,128)(2,1)S(1)}, u32[]{:S(2)}, u32[]{:S(2)}) %all-to-all-start.2) | async-done | bytes 524320 | tf_op jit(solution)/shard_map/all_to_all | solution.py:233
  (60 shorter events, 30.0 us)
Async XLA Ops:
  3.3 39.0 %collective-permute-start = (bf16[1536,512]{1,0:T(8,128)(2,1)}, bf16[1536,512]{1,0:T(8,128)(2,1)}, u32[]{:S(2)}, u32[]{:S(2)}) collective-permute-start(bf16[1536,512]{1,0:T(8,128)(2,1)} %pad_maximum_fusion), channel_id=1, source_target_pairs={{0,64},{64,0},{1,65},{65,1},{2,66},{66,2},{3,67},{67,3},{4,68},{68... | collective-permute-start | bytes 4718600 | tf_op jit(solution)/shard_map/ppermute | solution.py:42
  8.7 35.9 %all-to-all-start = ((bf16[16,32,1024]{2,1,0:T(8,128)(2,1)}), bf16[16,32,1024]{2,1,0:T(8,128)(2,1)S(1)}, u32[]{:S(2)}, u32[]{:S(2)}) async-start(bf16[16,32,1024]{2,1,0:T(8,128)(2,1)} %broadcast_in_dim.10), calls=%async_computation | async-start | bytes 2097152 | tf_op jit(solution)/shard_map/all_to_all | solution.py:152
  16.5 44.6 %copy-start = (bf16[512,512]{1,0:T(8,128)(2,1)S(1)}, bf16[512,512]{1,0:T(8,128)(2,1)}, u32[]{:S(2)}) copy-start(bf16[512,512]{1,0:T(8,128)(2,1)} %gate_w.3) | copy-start | bytes 1572868
  16.5 44.6 %copy-start.1 = (bf16[512,512]{1,0:T(8,128)(2,1)S(1)}, bf16[512,512]{1,0:T(8,128)(2,1)}, u32[]{:S(2)}) copy-start(bf16[512,512]{1,0:T(8,128)(2,1)} %up_w.3) | copy-start | bytes 1572868
  16.6 44.6 %copy-start.2 = (bf16[512,512]{1,0:T(8,128)(2,1)S(1)}, bf16[512,512]{1,0:T(8,128)(2,1)}, u32[]{:S(2)}) copy-start(bf16[512,512]{1,0:T(8,128)(2,1)} %down_w.1) | copy-start | bytes 1572868
  44.6 12.7 %collective-permute-start.2 = (bf16[2,128,1024]{2,1,0:T(8,128)(2,1)S(1)}, bf16[2,128,1024]{2,1,0:T(8,128)(2,1)S(1)}, u32[]{:S(2)}, u32[]{:S(2)}) collective-permute-start(bf16[2,128,1024]{2,1,0:T(8,128)(2,1)S(1)} %fusion.5), channel_id=1, source_target_pairs={{0,64},{64,0},{1,65},{65,1},{2,66},{66,2},{3,67},{67,3},{4,68},{68... | collective-permute-start | bytes 1572872 | tf_op jit(solution)/shard_map/ppermute | solution.py:42
  47.2 13.9 %collective-permute-start.1 = (bf16[2,2,128,1024]{3,2,1,0:T(8,128)(2,1)S(1)}, bf16[2,2,128,1024]{3,2,1,0:T(8,128)(2,1)S(1)}, u32[]{:S(2)}, u32[]{:S(2)}) collective-permute-start(bf16[2,2,128,1024]{3,2,1,0:T(8,128)(2,1)S(1)} %bitcast.11), channel_id=1, source_target_pairs={{0,1},{1,0},{2,3},{3,2},{4,5},{5,4},{6,7},{7,6},{8,9},{9,8},{10,11... | collective-permute-start | bytes 3145736 | tf_op jit(solution)/shard_map/ppermute | solution.py:42
  57.3 3.8 %collective-permute-start.3 = (bf16[256,1024]{1,0:T(8,128)(2,1)S(1)}, bf16[256,1024]{1,0:T(8,128)(2,1)S(1)}, u32[]{:S(2)}, u32[]{:S(2)}) collective-permute-start(bf16[256,1024]{1,0:T(8,128)(2,1)S(1)} %bitcast.19), channel_id=1, source_target_pairs={{0,1},{1,0},{2,3},{3,2},{4,5},{5,4},{6,7},{7,6},{8,9},{9,8},{10,11... | collective-permute-start | bytes 1572872 | tf_op jit(solution)/shard_map/ppermute | solution.py:42
  118.1 9.4 %collective-permute-start.6 = (bf16[64,1536]{1,0:T(8,128)(2,1)S(1)}, bf16[64,1536]{1,0:T(8,128)(2,1)S(1)}, u32[]{:S(2)}, u32[]{:S(2)}) collective-permute-start(bf16[64,1536]{1,0:T(8,128)(2,1)S(1)} %hidden_and_grads.1.trio_in), channel_id=1, source_target_pairs={{0,448},{64,0},{128,64},{192,128},{256,192},{320,256},{384,320},{4... | collective-permute-start | bytes 589832 | tf_op jit(solution)/shard_map/ppermute | solution.py:134
  120.7 12.0 %collective-permute-start.4 = (bf16[64,1536]{1,0:T(8,128)(2,1)S(1)}, bf16[64,1536]{1,0:T(8,128)(2,1)S(1)}, u32[]{:S(2)}, u32[]{:S(2)}) collective-permute-start(bf16[64,1536]{1,0:T(8,128)(2,1)S(1)} %hidden_and_grads.1.trio_in), channel_id=1, source_target_pairs={{0,64},{64,128},{128,192},{192,256},{256,320},{320,384},{384,448},... | collective-permute-start | bytes 589832 | tf_op jit(solution)/shard_map/ppermute | solution.py:134
  123.9 13.5 %collective-permute-start.8 = (bf16[64,1536]{1,0:T(8,128)(2,1)S(1)}, bf16[64,1536]{1,0:T(8,128)(2,1)S(1)}, u32[]{:S(2)}, u32[]{:S(2)}) collective-permute-start(bf16[64,1536]{1,0:T(8,128)(2,1)S(1)} %hidden_and_grads.1.trio_in), channel_id=1, source_target_pairs={{0,32},{32,0},{1,33},{33,1},{2,34},{34,2},{3,35},{35,3},{4,36},{36... | collective-permute-start | bytes 589832 | tf_op jit(solution)/shard_map/ppermute | solution.py:42
  127.5 10.6 %collective-permute-start.7 = (bf16[64,1536]{1,0:T(8,128)(2,1)S(1)}, bf16[64,1536]{1,0:T(8,128)(2,1)S(1)}, u32[]{:S(2)}, u32[]{:S(2)}) collective-permute-start(bf16[64,1536]{1,0:T(8,128)(2,1)S(1)} %collective-permute-done.6.refs_4_), channel_id=1, source_target_pairs={{0,448},{64,0},{128,64},{192,128},{256,192},{320,256},{384,320},{4... | collective-permute-start | bytes 589832 | tf_op jit(solution)/shard_map/ppermute | solution.py:134
  132.7 8.8 %collective-permute-start.5 = (bf16[64,1536]{1,0:T(8,128)(2,1)S(1)}, bf16[64,1536]{1,0:T(8,128)(2,1)S(1)}, u32[]{:S(2)}, u32[]{:S(2)}) collective-permute-start(bf16[64,1536]{1,0:T(8,128)(2,1)S(1)} %collective-permute-done.4.refs_0_), channel_id=1, source_target_pairs={{0,64},{64,128},{128,192},{192,256},{256,320},{320,384},{384,448},... | collective-permute-start | bytes 589832 | tf_op jit(solution)/shard_map/ppermute | solution.py:134
  134.6 17.5 %collective-permute-start.11 = (bf16[128,1536]{1,0:T(8,128)(2,1)S(1)}, bf16[128,1536]{1,0:T(8,128)(2,1)S(1)}, u32[]{:S(2)}, u32[]{:S(2)}) collective-permute-start(bf16[128,1536]{1,0:T(8,128)(2,1)S(1)} %pad_maximum_fusion.3), channel_id=1, source_target_pairs={{0,32},{32,0},{1,33},{33,1},{2,34},{34,2},{3,35},{35,3},{4,36},{36... | collective-permute-start | bytes 1179656 | tf_op jit(solution)/shard_map/ppermute | solution.py:42
  141.5 10.7 %collective-permute-start.9 = (bf16[64,1536]{1,0:T(8,128)(2,1)S(1)}, bf16[64,1536]{1,0:T(8,128)(2,1)S(1)}, u32[]{:S(2)}, u32[]{:S(2)}) collective-permute-start(bf16[64,1536]{1,0:T(8,128)(2,1)S(1)} %collective-permute-done.5.refs_1_), channel_id=1, source_target_pairs={{0,64},{64,128},{128,192},{192,256},{256,320},{320,384},{384,448},... | collective-permute-start | bytes 589832 | tf_op jit(solution)/shard_map/ppermute | solution.py:134
  143.4 8.7 %collective-permute-start.10 = (bf16[64,1536]{1,0:T(8,128)(2,1)S(1)}, bf16[64,1536]{1,0:T(8,128)(2,1)S(1)}, u32[]{:S(2)}, u32[]{:S(2)}) collective-permute-start(bf16[64,1536]{1,0:T(8,128)(2,1)S(1)} %collective-permute-done.7.refs_5_), channel_id=1, source_target_pairs={{0,448},{64,0},{128,64},{192,128},{256,192},{320,256},{384,320},{4... | collective-permute-start | bytes 589832 | tf_op jit(solution)/shard_map/ppermute | solution.py:134
  149.3 16.4 %collective-permute-start.13 = (bf16[128,1536]{1,0:T(8,128)(2,1)}, bf16[128,1536]{1,0:T(8,128)(2,1)}, u32[]{:S(2)}, u32[]{:S(2)}) collective-permute-start(bf16[128,1536]{1,0:T(8,128)(2,1)} %pad_maximum_fusion.4), channel_id=1, source_target_pairs={{0,32},{32,0},{1,33},{33,1},{2,34},{34,2},{3,35},{35,3},{4,36},{36... | collective-permute-start | bytes 1179656 | tf_op jit(solution)/shard_map/ppermute | solution.py:42
  152.2 8.9 %copy-start.5 = (bf16[128,1536]{1,0:T(8,128)(2,1)}, bf16[128,1536]{1,0:T(8,128)(2,1)S(1)}, u32[]{:S(2)}) copy-start(bf16[128,1536]{1,0:T(8,128)(2,1)S(1)} %collective-permute-done.11.refs_8_) | copy-start | bytes 1179652
  152.2 8.9 %collective-permute-start.12 = (bf16[64,1536]{1,0:T(8,128)(2,1)S(1)}, bf16[64,1536]{1,0:T(8,128)(2,1)}, u32[]{:S(2)}, u32[]{:S(2)}) collective-permute-start(bf16[64,1536]{1,0:T(8,128)(2,1)S(1)} %collective-permute-done.9.refs_2_), channel_id=1, source_target_pairs={{0,64},{64,128},{128,192},{192,256},{256,320},{320,384},{384,448},... | collective-permute-start | bytes 589832 | tf_op jit(solution)/shard_map/ppermute | solution.py:134
  154.9 19.0 %collective-permute-start.14 = (bf16[128,1536]{1,0:T(8,128)(2,1)}, bf16[128,1536]{1,0:T(8,128)(2,1)}, u32[]{:S(2)}, u32[]{:S(2)}) collective-permute-start(bf16[128,1536]{1,0:T(8,128)(2,1)} %pad_maximum_fusion.5), channel_id=1, source_target_pairs={{0,32},{32,0},{1,33},{33,1},{2,34},{34,2},{3,35},{35,3},{4,36},{36... | collective-permute-start | bytes 1179656 | tf_op jit(solution)/shard_map/ppermute | solution.py:42
  161.1 12.8 %collective-permute-start.15 = (bf16[64,1536]{1,0:T(8,128)(2,1)}, bf16[64,1536]{1,0:T(8,128)(2,1)}, u32[]{:S(2)}, u32[]{:S(2)}) collective-permute-start(bf16[64,1536]{1,0:T(8,128)(2,1)} %collective-permute-done.12.refs_3_), channel_id=1, source_target_pairs={{0,32},{32,0},{1,33},{33,1},{2,34},{34,2},{3,35},{35,3},{4,36},{36... | collective-permute-start | bytes 589832 | tf_op jit(solution)/shard_map/ppermute | solution.py:42
  180.1 13.5 %copy-start.4 = (bf16[2,2,128,1024]{3,2,1,0:T(8,128)(2,1)S(1)}, bf16[2,2,128,1024]{3,2,1,0:T(8,128)(2,1)}, u32[]{:S(2)}) copy-start(bf16[2,2,128,1024]{3,2,1,0:T(8,128)(2,1)} %copy-done.3) | copy-start | bytes 3145732
  180.1 4.7 %collective-permute-start.16 = (f32[512,512]{1,0:T(8,128)S(1)}, f32[512,512]{1,0:T(8,128)S(1)}, u32[]{:S(2)}, u32[]{:S(2)}) collective-permute-start(f32[512,512]{1,0:T(8,128)S(1)} %get-tuple-element.24), channel_id=1, source_target_pairs={{0,1},{1,0},{2,3},{3,2},{4,5},{5,4},{6,7},{7,6},{8,9},{9,8},{10,11... | collective-permute-start | bytes 3145736 | tf_op jit(solution)/shard_map/ppermute | solution.py:42
  185.7 25.8 %all-to-all-start.2 = ((bf16[16,32,512]{2,1,0:T(8,128)(2,1)}), bf16[16,32,512]{2,1,0:T(8,128)(2,1)S(1)}, u32[]{:S(2)}, u32[]{:S(2)}) async-start(bf16[16,32,512]{2,1,0:T(8,128)(2,1)} %bitcast.6), calls=%async_computation.2 | async-start | bytes 1048576 | tf_op jit(solution)/shard_map/all_to_all | solution.py:233
  (8 other events, 24.8 us)

commit v3 on v2

--- a/solution.py
+++ b/solution.py
@@ -92,42 +92,54 @@
             trio[:, at : at + LANES] = value
 
 
-def backward_kernel(zh_size, place, gate_w, up_w, trio_in, *refs):
+def backward_kernel(zh_size, gate_w, up_w, trio_in, *refs):
     size = 2 * zh_size
     rights, refs = refs[:zh_size], refs[zh_size:]
     lefts, refs = refs[: zh_size - 1], refs[zh_size - 1 :]
-    beside, (trio, in_own, in_other) = refs[: zh_size + 1], refs[zh_size + 1 :]
+    beside, (trio_out, in_own, in_other, trio, arrived, left) = refs[:zh_size], refs[zh_size:]
     rows, ff = trio_in.shape[0], gate_w.shape[1]
-    z, xh = place[0], place[1]
+    z, xh = 2 * lax.axis_index("zh") + lax.axis_index("zl"), lax.axis_index("xh")
+    copies = []
 
     def put(distance, mine, others):
-        at = 2 * rows * lax.rem(z + distance + size, size)
-        trio[pl.ds(pl.multiple_of(at + rows * xh, rows), rows), :] = mine
-        trio[pl.ds(pl.multiple_of(at + rows * (1 - xh), rows), rows), :] = others
-
-    put(0, trio_in[...], beside[0][...])
+        block = 2 * rows * lax.rem(z + distance + size, size)
+        for source, half in ((mine, xh), (others, 1 - xh)):
+            at = pl.multiple_of(block + rows * half, rows)
+            copies.append(
+                pltpu.make_async_copy(
+                    source, trio.at[pl.ds(at, rows), :], arrived.at[len(copies)]
+                )
+            )
+            copies[-1].start()
+
+    put(0, trio_in, beside[0].at[pl.ds(0, rows), :])
     for k in range(1, zh_size):
-        put(-k, rights[k - 1][...], beside[k][:rows, :])
-        put(k, lefts[k - 1][...], beside[k][rows:, :])
-    put(-zh_size, rights[-1][...], beside[-1][...])
+        others = beside[k - 1]
+        at = others.shape[0] - 2 * rows
+        put(-k, rights[k - 1], others.at[pl.ds(at, rows), :])
+        put(k, lefts[k - 1], others.at[pl.ds(at + rows, rows), :])
+    put(-zh_size, rights[-1], beside[-1])
+    for copy in copies:
+        copy.wait()
+    copy = pltpu.make_async_copy(trio, trio_out, left)
+    copy.start()
     share = in_own.shape[0]
     for part, target in ((1, in_other), (0, in_own)):
         at = slice(part * share, (part + 1) * share)
         target[...] = contract_cols(trio[at, ff : 2 * ff], gate_w[...]) + contract_cols(
             trio[at, 2 * ff :], up_w[...]
         )
-
-
-def early(x):
-    return pl.pallas_call(
-        lambda x_ref, out_ref: None,
-        out_shape=jax.ShapeDtypeStruct(x.shape, x.dtype),
-        in_specs=[pl.BlockSpec(memory_space=pltpu.HBM)],
-        out_specs=pl.BlockSpec(memory_space=pltpu.HBM),
-        input_output_aliases={0: 0},
-        cost_estimate=pl.CostEstimate(flops=10**11, bytes_accessed=0, transcendentals=0),
-        name="exchanged",
-    )(x)
+    copy.wait()
+
+
+def pair_swap(x, zh_size):
+    size = 2 * zh_size
+    pairs = [
+        (2 * z + c, 2 * ((z + (1 if z % 2 == c else -1)) % size) + c)
+        for z in range(size)
+        for c in range(2)
+    ]
+    return lax.ppermute(x, ("zh", "zl", "c"), pairs)
 
 
 def turn(x, size, step):
@@ -146,17 +158,17 @@
     ff = gate_weight.shape[1]
     group = 2 * zh_size
 
-    far = swap(jnp.concatenate([gate_weight, up_weight, down_weight], axis=0), "zl")
+    far = pair_swap(jnp.concatenate([gate_weight, up_weight, down_weight], axis=0), zh_size)
 
     shard = jnp.concatenate([tokens, out_grad], axis=1)
     own = lax.all_to_all(
         jnp.broadcast_to(shard[None], (blocks, rows, 2 * depth)), ("y", "xl"), 0, 0, tiled=True
     )
-    own, far = lax.optimization_barrier((own, early(far)))
+    own, far = lax.optimization_barrier((own, far))
     own = own.reshape(zh_size // 2, 2, -1, 2 * depth)
-    ext = swap(pick(~first, own), "zl").reshape(-1, 2 * depth)
     other = swap(own, "c")
-    ext_other = swap(ext, "c")
+    ext = pair_swap(pick(~first, own), zh_size).reshape(-1, 2 * depth)
+    ext_other = pair_swap(pick(~first, other), zh_size).reshape(-1, 2 * depth)
 
     half_tokens = own.size // (2 * depth)
     token_rows = half_tokens // group
@@ -193,20 +205,22 @@
         name="hidden_and_grads",
     )(parts.astype(jnp.float32))
 
-    right, left = [trio], [trio]
-    beside = [swap(trio, "xh")]
+    right, left, beside = [trio], [trio], []
+    waiting = [trio]
     for step in range(1, zh_size):
         right.append(turn(right[-1], 2 * zh_size, 1))
         left.append(turn(left[-1], 2 * zh_size, -1))
-        if step >= 2:
-            right[-1], left[-1], beside[step - 2] = lax.optimization_barrier(
-                (right[-1], left[-1], beside[step - 2])
+        waiting = waiting + [right[-1], left[-1]]
+        if step >= 3:
+            right[-1], left[-1], beside[step - 3] = lax.optimization_barrier(
+                (right[-1], left[-1], beside[step - 3])
             )
-        beside.append(swap(jnp.concatenate([right[-1], left[-1]], axis=0), "xh"))
+            waiting = [right[-1], left[-1]]
+        beside.append(swap(jnp.concatenate(waiting, axis=0), "xh"))
+        waiting = []
     right.append(turn(right[-1], 2 * zh_size, 1))
     beside.append(swap(right[-1], "xh"))
 
-    place = jnp.stack([2 * lax.axis_index("zh") + zl, xh]).astype(jnp.int32)
     blocks_in = [trio] + right[1:] + left[1:] + beside
     share = half_tokens
     trio, in_own, in_other = pl.pallas_call(
@@ -216,15 +230,21 @@
             jax.ShapeDtypeStruct((share, depth), jnp.float32),
             jax.ShapeDtypeStruct((share, depth), jnp.float32),
         ),
-        in_specs=[pl.BlockSpec(memory_space=pltpu.SMEM)]
-        + [pl.BlockSpec(memory_space=pltpu.VMEM)] * (2 + len(blocks_in)),
-        out_specs=[pl.BlockSpec(memory_space=pltpu.VMEM)] * 3,
+        in_specs=[pl.BlockSpec(memory_space=pltpu.VMEM)] * 2
+        + [pl.BlockSpec(memory_space=pltpu.HBM)] * len(blocks_in),
+        out_specs=[pl.BlockSpec(memory_space=pltpu.HBM)]
+        + [pl.BlockSpec(memory_space=pltpu.VMEM)] * 2,
+        scratch_shapes=[
+            pltpu.VMEM((2 * share, 3 * ff), jnp.bfloat16),
+            pltpu.SemaphoreType.DMA((4 * zh_size,)),
+            pltpu.SemaphoreType.DMA,
+        ],
         compiler_params=pltpu.CompilerParams(vmem_limit_bytes=40 * 2**20),
         cost_estimate=pl.CostEstimate(
             flops=8 * share * depth * ff, bytes_accessed=9 * 2**20, transcendentals=0
         ),
         name="input_gradient",
-    )(place, gate_weight, up_weight, *blocks_in)
+    )(gate_weight, up_weight, *blocks_in)
     hidden, gate_grad, up_grad = trio[:, :ff], trio[:, ff : 2 * ff], trio[:, 2 * ff :]
 
     every = jnp.concatenate([x.reshape(-1, 2 * depth) for x in (own, other)], axis=0)

time: 213 us -> 206 us (0.967)
  starting transfers between devices: 68.4 us -> 57.8 us
  waiting for transfers between devices: 65.8 us -> 72.2 us
  other arithmetic: 6.4 us -> 3.27 us
    ppermute x10 -> x6, waiting for transfers between devices: 46.5 us -> 9.75 us  [swap(): return lax.ppermute(x, axis, [(0, 1), (1, 0)])]
    ppermute x0 -> x3, waiting for transfers between devices: none -> 29.1 us  [pair_swap(): return lax.ppermute(x, ('zh', 'zl', 'c'), pairs)]
    ppermute x10 -> x6, starting transfers between devices: 30.9 us -> 16.7 us  [swap(): return lax.ppermute(x, axis, [(0, 1), (1, 0)])]
    ppermute x7, waiting for transfers between devices: 5 us -> 16.1 us  [turn(): lax.ppermute(x, ('zh', 'zl'), [(i, (i + step) % size) for i in range(size)])]
    ppermute x0 -> x3, starting transfers between devices: none -> 10.3 us  [pair_swap(): return lax.ppermute(x, ('zh', 'zl', 'c'), pairs)]
    all_to_all x1, starting transfers between devices: 7.84 us -> 3.57 us  [per_device(): lax.all_to_all(in_part.astype(jnp.bfloat16).reshape(blocks, rows, depth),...]
    pallas_call x1, Pallas kernels: 2.71 us -> 5.79 us  [per_device(): pl.pallas_call(functools.partial(backward_kernel, zh_size), out_shape=(ja...]
    concatenate x1, other arithmetic: 2.61 us -> 0.1 us  [per_device(): jnp.concatenate([gate_weight, up_weight, down_weight], axis=0)]
  transfers between devices with their start and end apart: 19 -> 18, of which waited for: 9 -> 12; matrix products, arithmetic and copies ran while one was open for 4% -> 3% of each run, Pallas kernels for 0% -> 0%
where the time goes in v3:
time: 206 us; the launch traced here: 205 us
  waiting for transfers between devices  72.2 us (35%)
  starting transfers between devices  57.8 us (28%)
  blocking collectives  52.8 us (26%)
  Pallas kernels  8.13 us (4%)
  matrix products  5.97 us (3%)
  local copies, waits for them, and re-layouts  3.93 us (2%)
  other arithmetic  3.27 us (2%)
    all_to_all x1, blocking collectives, per_device(): lax.all_to_all(parts.astype(jnp.float16), ('zh', 'xh'), 0, 0, tiled=True)  52.8 us
    ppermute x3, waiting for transfers between devices, pair_swap(): return lax.ppermute(x, ('zh', 'zl', 'c'), pairs)  29.1 us
    ppermute x7, starting transfers between devices, turn(): lax.ppermute(x, ('zh', 'zl'), [(i, (i + step) % size) for i in range(size)])  19.4 us
    ppermute x6, starting transfers between devices, swap(): return lax.ppermute(x, axis, [(0, 1), (1, 0)])  16.7 us
    ppermute x7, waiting for transfers between devices, turn(): lax.ppermute(x, ('zh', 'zl'), [(i, (i + step) % size) for i in range(size)])  16.1 us
    all_to_all x1, waiting for transfers between devices, per_device(): lax.all_to_all(in_part.astype(jnp.bfloat16).reshape(blocks, rows, depth),...  12.5 us
    ppermute x3, starting transfers between devices, pair_swap(): return lax.ppermute(x, ('zh', 'zl', 'c'), pairs)  10.3 us
    ppermute x6, waiting for transfers between devices, swap(): return lax.ppermute(x, axis, [(0, 1), (1, 0)])  9.75 us
  transfers between devices with their start and end apart: 18, of which 12 were waited for; matrix products, arithmetic and copies ran while one was open for 3% of the time, Pallas kernels for 0%

profile of v3, /device:TPU:4, one launch (start us, length us, event | category | flops | bytes accessed | tf_op | source)
XLA Modules:
  0.0 205.0 jit_solution(6903583902343161332)
XLA Ops:
  2.7 7.8 %all-to-all-start = ((bf16[16,32,1024]{2,1,0:T(8,128)(2,1)}), bf16[16,32,1024]{2,1,0:T(8,128)(2,1)S(1)}, u32[]{:S(2)}, u32[]{:S(2)}) async-start(bf16[16,32,1024]{2,1,0:T(8,128)(2,1)} %broadcast_in_dim.10), calls=%async_computation | async-start | bytes 2097152 | tf_op jit(solution)/shard_map/all_to_all | solution.py:164
  10.6 4.3 %collective-permute-start = (bf16[1536,512]{1,0:T(8,128)(2,1)S(1)}, bf16[1536,512]{1,0:T(8,128)(2,1)S(1)}, u32[]{:S(2)}, u32[]{:S(2)}) collective-permute-start(bf16[1536,512]{1,0:T(8,128)(2,1)S(1)} %pad_maximum_fusion), channel_id=1, source_target_pairs={{0,64},{1,449},{64,0},{65,129},{128,192},{129,65},{192,128},{193,2... | collective-permute-start | bytes 4718600 | tf_op jit(solution)/shard_map/ppermute | solution.py:142
  14.9 18.4 %collective-permute-done.far = bf16[1536,512]{1,0:T(8,128)(2,1)S(1)} collective-permute-done((bf16[1536,512]{1,0:T(8,128)(2,1)S(1)}, bf16[1536,512]{1,0:T(8,128)(2,1)S(1)}, u32[]{:S(2)}, u32[]{:S(2)}) %collective-permute-start) | collective-permute-done | bytes 1572896 | tf_op jit(solution)/shard_map/ppermute | solution.py:142
  34.5 4.7 %all-to-all-done = bf16[16,32,1024]{2,1,0:T(8,128)(2,1)S(1)} async-done(((bf16[16,32,1024]{2,1,0:T(8,128)(2,1)}), bf16[16,32,1024]{2,1,0:T(8,128)(2,1)S(1)}, u32[]{:S(2)}, u32[]{:S(2)}) %all-to-all-start) | async-done | bytes 1048608 | tf_op jit(solution)/shard_map/all_to_all | solution.py:164
  39.2 2.9 %collective-permute-start.1 = (bf16[2,2,128,1024]{3,2,1,0:T(8,128)(2,1)S(1)}, bf16[2,2,128,1024]{3,2,1,0:T(8,128)(2,1)S(1)}, u32[]{:S(2)}, u32[]{:S(2)}) collective-permute-start(bf16[2,2,128,1024]{3,2,1,0:T(8,128)(2,1)S(1)} %bitcast.11), channel_id=1, source_target_pairs={{0,1},{1,0},{2,3},{3,2},{4,5},{5,4},{6,7},{7,6},{8,9},{9,8},{10,11... | collective-permute-start | bytes 3145736 | tf_op jit(solution)/shard_map/ppermute | solution.py:42
  42.2 3.5 %collective-permute-start.2 = (bf16[2,128,1024]{2,1,0:T(8,128)(2,1)S(1)}, bf16[2,128,1024]{2,1,0:T(8,128)(2,1)S(1)}, u32[]{:S(2)}, u32[]{:S(2)}) collective-permute-start(bf16[2,128,1024]{2,1,0:T(8,128)(2,1)S(1)} %fusion.6), channel_id=1, source_target_pairs={{0,64},{1,449},{64,0},{65,129},{128,192},{129,65},{192,128},{193,2... | collective-permute-start | bytes 1572872 | tf_op jit(solution)/shard_map/ppermute | solution.py:142
  48.2 5.1 %collective-permute-done.2 = bf16[2,128,1024]{2,1,0:T(8,128)(2,1)S(1)} collective-permute-done((bf16[2,128,1024]{2,1,0:T(8,128)(2,1)S(1)}, bf16[2,128,1024]{2,1,0:T(8,128)(2,1)S(1)}, u32[]{:S(2)}, u32[]{:S(2)}) %collective-permute-start.2) | collective-permute-done | bytes 524320 | tf_op jit(solution)/shard_map/ppermute | solution.py:142
  53.4 5.6 %collective-permute-done.3 = bf16[2,128,1024]{2,1,0:T(8,128)(2,1)S(1)} collective-permute-done((bf16[2,128,1024]{2,1,0:T(8,128)(2,1)S(1)}, bf16[2,128,1024]{2,1,0:T(8,128)(2,1)S(1)}, u32[]{:S(2)}, u32[]{:S(2)}) %collective-permute-start.3) | collective-permute-done | bytes 524320 | tf_op jit(solution)/shard_map/ppermute | solution.py:142
  61.3 52.8 %all_to_all.15 = f16[8,784,128]{2,1,0:T(8,128)(2,1)S(1)} all-to-all(f16[8,784,128]{2,1,0:T(8,128)(2,1)S(1)} %convert_element_type.20), channel_id=1, replica_groups=mesh['zh'=4,'zl'=2,'xh'=2,'y'=8,'xl'=2,'c'=2] {'zh','xh'}, dimensions={0} | all-to-all | bytes 3211264 | tf_op jit(solution)/shard_map/all_to_all | solution.py:193
  114.6 2.6 %collective-permute-start.7 = (bf16[64,1536]{1,0:T(8,128)(2,1)S(1)}, bf16[64,1536]{1,0:T(8,128)(2,1)S(1)}, u32[]{:S(2)}, u32[]{:S(2)}) collective-permute-start(bf16[64,1536]{1,0:T(8,128)(2,1)S(1)} %hidden_and_grads.1.trio_in), channel_id=1, source_target_pairs={{0,448},{64,0},{128,64},{192,128},{256,192},{320,256},{384,320},{4... | collective-permute-start | bytes 589832 | tf_op jit(solution)/shard_map/ppermute | solution.py:146
  117.1 3.3 %collective-permute-start.4 = (bf16[64,1536]{1,0:T(8,128)(2,1)S(1)}, bf16[64,1536]{1,0:T(8,128)(2,1)S(1)}, u32[]{:S(2)}, u32[]{:S(2)}) collective-permute-start(bf16[64,1536]{1,0:T(8,128)(2,1)S(1)} %hidden_and_grads.1.trio_in), channel_id=1, source_target_pairs={{0,64},{64,128},{128,192},{192,256},{256,320},{320,384},{384,448},... | collective-permute-start | bytes 589832 | tf_op jit(solution)/shard_map/ppermute | solution.py:146
  122.1 4.5 %collective-permute-done.4.refs_0_ = bf16[64,1536]{1,0:T(8,128)(2,1)S(1)} collective-permute-done((bf16[64,1536]{1,0:T(8,128)(2,1)S(1)}, bf16[64,1536]{1,0:T(8,128)(2,1)S(1)}, u32[]{:S(2)}, u32[]{:S(2)}) %collective-permute-start.4) | collective-permute-done | bytes 196640 | tf_op jit(solution)/shard_map/ppermute | solution.py:146
  126.7 5.1 %collective-permute-start.10 = (bf16[192,1536]{1,0:T(8,128)(2,1)S(1)}, bf16[192,1536]{1,0:T(8,128)(2,1)S(1)}, u32[]{:S(2)}, u32[]{:S(2)}) collective-permute-start(bf16[192,1536]{1,0:T(8,128)(2,1)S(1)} %pad_maximum_fusion.3), channel_id=1, source_target_pairs={{0,32},{32,0},{1,33},{33,1},{2,34},{34,2},{3,35},{35,3},{4,36},{36... | collective-permute-start | bytes 1769480 | tf_op jit(solution)/shard_map/ppermute | solution.py:42
  133.6 3.9 %collective-permute-start.5 = (bf16[64,1536]{1,0:T(8,128)(2,1)S(1)}, bf16[64,1536]{1,0:T(8,128)(2,1)S(1)}, u32[]{:S(2)}, u32[]{:S(2)}) collective-permute-start(bf16[64,1536]{1,0:T(8,128)(2,1)S(1)} %collective-permute-done.4.refs_0_), channel_id=1, source_target_pairs={{0,64},{64,128},{128,192},{192,256},{256,320},{320,384},{384,448},... | collective-permute-start | bytes 589832 | tf_op jit(solution)/shard_map/ppermute | solution.py:146
  139.3 3.1 %collective-permute-start.9 = (bf16[64,1536]{1,0:T(8,128)(2,1)S(1)}, bf16[64,1536]{1,0:T(8,128)(2,1)S(1)}, u32[]{:S(2)}, u32[]{:S(2)}) collective-permute-start(bf16[64,1536]{1,0:T(8,128)(2,1)S(1)} %collective-permute-done.8.refs_5_), channel_id=1, source_target_pairs={{0,448},{64,0},{128,64},{192,128},{256,192},{320,256},{384,320},{4... | collective-permute-start | bytes 589832 | tf_op jit(solution)/shard_map/ppermute | solution.py:146
  142.4 2.7 %collective-permute-start.6 = (bf16[64,1536]{1,0:T(8,128)(2,1)S(1)}, bf16[64,1536]{1,0:T(8,128)(2,1)S(1)}, u32[]{:S(2)}, u32[]{:S(2)}) collective-permute-start(bf16[64,1536]{1,0:T(8,128)(2,1)S(1)} %collective-permute-done.5.refs_1_), channel_id=1, source_target_pairs={{0,64},{64,128},{128,192},{192,256},{256,320},{320,384},{384,448},... | collective-permute-start | bytes 589832 | tf_op jit(solution)/shard_map/ppermute | solution.py:146
  147.5 3.7 %collective-permute-done.6.refs_2_ = bf16[64,1536]{1,0:T(8,128)(2,1)S(1)} collective-permute-done((bf16[64,1536]{1,0:T(8,128)(2,1)S(1)}, bf16[64,1536]{1,0:T(8,128)(2,1)S(1)}, u32[]{:S(2)}, u32[]{:S(2)}) %collective-permute-start.6) | collective-permute-done | bytes 196640 | tf_op jit(solution)/shard_map/ppermute | solution.py:146
  155.5 4.5 %collective-permute-done.11.refs_3_ = bf16[64,1536]{1,0:T(8,128)(2,1)S(1)} collective-permute-done((bf16[64,1536]{1,0:T(8,128)(2,1)S(1)}, bf16[64,1536]{1,0:T(8,128)(2,1)S(1)}, u32[]{:S(2)}, u32[]{:S(2)}) %collective-permute-start.11) | collective-permute-done | bytes 196640 | tf_op jit(solution)/shard_map/ppermute | solution.py:146
  162.3 7.1 %collective-permute-done.14.refs_10_ = bf16[64,1536]{1,0:T(8,128)(2,1)S(1)} collective-permute-done((bf16[64,1536]{1,0:T(8,128)(2,1)S(1)}, bf16[64,1536]{1,0:T(8,128)(2,1)S(1)}, u32[]{:S(2)}, u32[]{:S(2)}) %collective-permute-start.14) | collective-permute-done | bytes 196640 | tf_op jit(solution)/shard_map/ppermute | solution.py:42
  169.4 5.8 %input_gradient.1 = (bf16[1024,1536]{1,0:T(8,128)(2,1)S(1)}, f32[512,512]{1,0:T(8,128)S(1)}, f32[512,512]{1,0:T(8,128)S(1)}) custom-call(bf16[512,512]{1,0:T(8,128)(2,1)S(1)} %copy-done, bf16[512,512]{1,0:T(8,128)(2,1)S(1)} %copy-done.1, bf16[64,1536]{1,0:T(8,128)(2,1)S(1)} %hidden_and_grads.1.trio_in, bf16[64,1536]{1,0:T(8,128)(2,1)S(1)} %collective-permute-done.4.refs_0_, ...), custom_call_target="tpu_custom_call" | custom-call | flops 1073741824 | bytes 9437184 | tf_op jit(solution)/shard_map/input_gradient/pallas_call | solution.py:226
  178.7 2.6 %collective-permute-done.15 = f32[512,512]{1,0:T(8,128)S(1)} collective-permute-done((f32[512,512]{1,0:T(8,128)S(1)}, f32[512,512]{1,0:T(8,128)S(1)}, u32[]{:S(2)}, u32[]{:S(2)}) %collective-permute-start.15) | collective-permute-done | bytes 1048608 | tf_op jit(solution)/shard_map/ppermute | solution.py:42
  182.3 3.6 %all-to-all-start.2 = ((bf16[16,32,512]{2,1,0:T(8,128)(2,1)}), bf16[16,32,512]{2,1,0:T(8,128)(2,1)S(1)}, u32[]{:S(2)}, u32[]{:S(2)}) async-start(bf16[16,32,512]{2,1,0:T(8,128)(2,1)} %bitcast.6), calls=%async_computation.2 | async-start | bytes 1048576 | tf_op jit(solution)/shard_map/all_to_all | solution.py:253
  185.9 2.9 %convolution_convert_fusion = bf16[512,512]{1,0:T(8,128)(2,1)} fusion(bf16[512,1024]{1,0:T(8,128)(2,1)S(1)} %bitcast.17, bf16[512,1024]{1,0:T(8,128)(2,1)S(1)} %bitcast.14, bf16[1024,1536]{1,0:T(8,128)(2,1)} %copy-done.6), kind=kOutput, calls=%fused_computation.3 | convolution fusion | flops 539230208 | bytes 3670016 | tf_op jit(solution)/shard_map/dot_general | solution.py:26
  191.9 12.5 %all-to-all-done.2 = bf16[16,32,512]{2,1,0:T(8,128)(2,1)S(1)} async-done(((bf16[16,32,512]{2,1,0:T(8,128)(2,1)}), bf16[16,32,512]{2,1,0:T(8,128)(2,1)S(1)}, u32[]{:S(2)}, u32[]{:S(2)}) %all-to-all-start.2) | async-done | bytes 524320 | tf_op jit(solution)/shard_map/all_to_all | solution.py:253
  (47 shorter events, 31.2 us)
Async XLA Ops:
  0.6 9.9 %copy-start.1 = (bf16[512,512]{1,0:T(8,128)(2,1)S(1)}, bf16[512,512]{1,0:T(8,128)(2,1)}, u32[]{:S(2)}) copy-start(bf16[512,512]{1,0:T(8,128)(2,1)} %up_w.3) | copy-start | bytes 1572868
  0.6 9.9 %copy-start = (bf16[512,512]{1,0:T(8,128)(2,1)S(1)}, bf16[512,512]{1,0:T(8,128)(2,1)}, u32[]{:S(2)}) copy-start(bf16[512,512]{1,0:T(8,128)(2,1)} %gate_w.3) | copy-start | bytes 1572868
  0.7 9.9 %copy-start.2 = (bf16[512,512]{1,0:T(8,128)(2,1)S(1)}, bf16[512,512]{1,0:T(8,128)(2,1)}, u32[]{:S(2)}) copy-start(bf16[512,512]{1,0:T(8,128)(2,1)} %down_w.1) | copy-start | bytes 1572868
  2.7 36.5 %all-to-all-start = ((bf16[16,32,1024]{2,1,0:T(8,128)(2,1)}), bf16[16,32,1024]{2,1,0:T(8,128)(2,1)S(1)}, u32[]{:S(2)}, u32[]{:S(2)}) async-start(bf16[16,32,1024]{2,1,0:T(8,128)(2,1)} %broadcast_in_dim.10), calls=%async_computation | async-start | bytes 2097152 | tf_op jit(solution)/shard_map/all_to_all | solution.py:164
  10.6 22.7 %collective-permute-start = (bf16[1536,512]{1,0:T(8,128)(2,1)S(1)}, bf16[1536,512]{1,0:T(8,128)(2,1)S(1)}, u32[]{:S(2)}, u32[]{:S(2)}) collective-permute-start(bf16[1536,512]{1,0:T(8,128)(2,1)S(1)} %pad_maximum_fusion), channel_id=1, source_target_pairs={{0,64},{1,449},{64,0},{65,129},{128,192},{129,65},{192,128},{193,2... | collective-permute-start | bytes 4718600 | tf_op jit(solution)/shard_map/ppermute | solution.py:142
  39.2 6.4 %collective-permute-start.1 = (bf16[2,2,128,1024]{3,2,1,0:T(8,128)(2,1)S(1)}, bf16[2,2,128,1024]{3,2,1,0:T(8,128)(2,1)S(1)}, u32[]{:S(2)}, u32[]{:S(2)}) collective-permute-start(bf16[2,2,128,1024]{3,2,1,0:T(8,128)(2,1)S(1)} %bitcast.11), channel_id=1, source_target_pairs={{0,1},{1,0},{2,3},{3,2},{4,5},{5,4},{6,7},{7,6},{8,9},{9,8},{10,11... | collective-permute-start | bytes 3145736 | tf_op jit(solution)/shard_map/ppermute | solution.py:42
  42.1 16.9 %copy-start.3 = (bf16[512,512]{1,0:T(8,128)(2,1)S(1)}, bf16[512,512]{1,0:T(8,128)(2,1)}, u32[]{:S(2)}) copy-start(bf16[512,512]{1,0:T(8,128)(2,1)} %down_w.1) | copy-start | bytes 1572868
  42.1 16.9 %copy-start.5 = (bf16[1536,512]{1,0:T(8,128)(2,1)S(1)}, bf16[1536,512]{1,0:T(8,128)(2,1)}, u32[]{:S(2)}) copy-start(bf16[1536,512]{1,0:T(8,128)(2,1)} %copy-done.4) | copy-start | bytes 4718596
  42.2 11.2 %collective-permute-start.2 = (bf16[2,128,1024]{2,1,0:T(8,128)(2,1)S(1)}, bf16[2,128,1024]{2,1,0:T(8,128)(2,1)S(1)}, u32[]{:S(2)}, u32[]{:S(2)}) collective-permute-start(bf16[2,128,1024]{2,1,0:T(8,128)(2,1)S(1)} %fusion.6), channel_id=1, source_target_pairs={{0,64},{1,449},{64,0},{65,129},{128,192},{129,65},{192,128},{193,2... | collective-permute-start | bytes 1572872 | tf_op jit(solution)/shard_map/ppermute | solution.py:142
  45.7 13.3 %collective-permute-start.3 = (bf16[2,128,1024]{2,1,0:T(8,128)(2,1)S(1)}, bf16[2,128,1024]{2,1,0:T(8,128)(2,1)S(1)}, u32[]{:S(2)}, u32[]{:S(2)}) collective-permute-start(bf16[2,128,1024]{2,1,0:T(8,128)(2,1)S(1)} %fusion.5), channel_id=1, source_target_pairs={{0,64},{1,449},{64,0},{65,129},{128,192},{129,65},{192,128},{193,2... | collective-permute-start | bytes 1572872 | tf_op jit(solution)/shard_map/ppermute | solution.py:142
  114.6 7.6 %collective-permute-start.7 = (bf16[64,1536]{1,0:T(8,128)(2,1)S(1)}, bf16[64,1536]{1,0:T(8,128)(2,1)S(1)}, u32[]{:S(2)}, u32[]{:S(2)}) collective-permute-start(bf16[64,1536]{1,0:T(8,128)(2,1)S(1)} %hidden_and_grads.1.trio_in), channel_id=1, source_target_pairs={{0,448},{64,0},{128,64},{192,128},{256,192},{320,256},{384,320},{4... | collective-permute-start | bytes 589832 | tf_op jit(solution)/shard_map/ppermute | solution.py:146
  117.1 9.5 %collective-permute-start.4 = (bf16[64,1536]{1,0:T(8,128)(2,1)S(1)}, bf16[64,1536]{1,0:T(8,128)(2,1)S(1)}, u32[]{:S(2)}, u32[]{:S(2)}) collective-permute-start(bf16[64,1536]{1,0:T(8,128)(2,1)S(1)} %hidden_and_grads.1.trio_in), channel_id=1, source_target_pairs={{0,64},{64,128},{128,192},{192,256},{256,320},{320,384},{384,448},... | collective-permute-start | bytes 589832 | tf_op jit(solution)/shard_map/ppermute | solution.py:146
  126.7 24.5 %collective-permute-start.10 = (bf16[192,1536]{1,0:T(8,128)(2,1)S(1)}, bf16[192,1536]{1,0:T(8,128)(2,1)S(1)}, u32[]{:S(2)}, u32[]{:S(2)}) collective-permute-start(bf16[192,1536]{1,0:T(8,128)(2,1)S(1)} %pad_maximum_fusion.3), channel_id=1, source_target_pairs={{0,32},{32,0},{1,33},{33,1},{2,34},{34,2},{3,35},{35,3},{4,36},{36... | collective-permute-start | bytes 1769480 | tf_op jit(solution)/shard_map/ppermute | solution.py:42
  131.7 7.6 %collective-permute-start.8 = (bf16[64,1536]{1,0:T(8,128)(2,1)S(1)}, bf16[64,1536]{1,0:T(8,128)(2,1)S(1)}, u32[]{:S(2)}, u32[]{:S(2)}) collective-permute-start(bf16[64,1536]{1,0:T(8,128)(2,1)S(1)} %collective-permute-done.7.refs_4_), channel_id=1, source_target_pairs={{0,448},{64,0},{128,64},{192,128},{256,192},{320,256},{384,320},{4... | collective-permute-start | bytes 589832 | tf_op jit(solution)/shard_map/ppermute | solution.py:146
  133.6 8.8 %collective-permute-start.5 = (bf16[64,1536]{1,0:T(8,128)(2,1)S(1)}, bf16[64,1536]{1,0:T(8,128)(2,1)S(1)}, u32[]{:S(2)}, u32[]{:S(2)}) collective-permute-start(bf16[64,1536]{1,0:T(8,128)(2,1)S(1)} %collective-permute-done.4.refs_0_), channel_id=1, source_target_pairs={{0,64},{64,128},{128,192},{192,256},{256,320},{320,384},{384,448},... | collective-permute-start | bytes 589832 | tf_op jit(solution)/shard_map/ppermute | solution.py:146
  139.3 8.2 %collective-permute-start.9 = (bf16[64,1536]{1,0:T(8,128)(2,1)S(1)}, bf16[64,1536]{1,0:T(8,128)(2,1)S(1)}, u32[]{:S(2)}, u32[]{:S(2)}) collective-permute-start(bf16[64,1536]{1,0:T(8,128)(2,1)S(1)} %collective-permute-done.8.refs_5_), channel_id=1, source_target_pairs={{0,448},{64,0},{128,64},{192,128},{256,192},{320,256},{384,320},{4... | collective-permute-start | bytes 589832 | tf_op jit(solution)/shard_map/ppermute | solution.py:146
  142.4 8.8 %collective-permute-start.6 = (bf16[64,1536]{1,0:T(8,128)(2,1)S(1)}, bf16[64,1536]{1,0:T(8,128)(2,1)S(1)}, u32[]{:S(2)}, u32[]{:S(2)}) collective-permute-start(bf16[64,1536]{1,0:T(8,128)(2,1)S(1)} %collective-permute-done.5.refs_1_), channel_id=1, source_target_pairs={{0,64},{64,128},{128,192},{192,256},{256,320},{320,384},{384,448},... | collective-permute-start | bytes 589832 | tf_op jit(solution)/shard_map/ppermute | solution.py:146
  145.2 17.1 %collective-permute-start.12 = (bf16[128,1536]{1,0:T(8,128)(2,1)S(1)}, bf16[128,1536]{1,0:T(8,128)(2,1)S(1)}, u32[]{:S(2)}, u32[]{:S(2)}) collective-permute-start(bf16[128,1536]{1,0:T(8,128)(2,1)S(1)} %pad_maximum_fusion.4), channel_id=1, source_target_pairs={{0,32},{32,0},{1,33},{33,1},{2,34},{34,2},{3,35},{35,3},{4,36},{36... | collective-permute-start | bytes 1179656 | tf_op jit(solution)/shard_map/ppermute | solution.py:42
  151.2 8.8 %collective-permute-start.11 = (bf16[64,1536]{1,0:T(8,128)(2,1)S(1)}, bf16[64,1536]{1,0:T(8,128)(2,1)S(1)}, u32[]{:S(2)}, u32[]{:S(2)}) collective-permute-start(bf16[64,1536]{1,0:T(8,128)(2,1)S(1)} %collective-permute-done.6.refs_2_), channel_id=1, source_target_pairs={{0,64},{64,128},{128,192},{192,256},{256,320},{320,384},{384,448},... | collective-permute-start | bytes 589832 | tf_op jit(solution)/shard_map/ppermute | solution.py:146
  153.2 16.2 %collective-permute-start.13 = (bf16[128,1536]{1,0:T(8,128)(2,1)S(1)}, bf16[128,1536]{1,0:T(8,128)(2,1)S(1)}, u32[]{:S(2)}, u32[]{:S(2)}) collective-permute-start(bf16[128,1536]{1,0:T(8,128)(2,1)S(1)} %pad_maximum_fusion.5), channel_id=1, source_target_pairs={{0,32},{32,0},{1,33},{33,1},{2,34},{34,2},{3,35},{35,3},{4,36},{36... | collective-permute-start | bytes 1179656 | tf_op jit(solution)/shard_map/ppermute | solution.py:42
  160.0 9.4 %collective-permute-start.14 = (bf16[64,1536]{1,0:T(8,128)(2,1)S(1)}, bf16[64,1536]{1,0:T(8,128)(2,1)S(1)}, u32[]{:S(2)}, u32[]{:S(2)}) collective-permute-start(bf16[64,1536]{1,0:T(8,128)(2,1)S(1)} %collective-permute-done.11.refs_3_), channel_id=1, source_target_pairs={{0,32},{32,0},{1,33},{33,1},{2,34},{34,2},{3,35},{35,3},{4,36},{36... | collective-permute-start | bytes 589832 | tf_op jit(solution)/shard_map/ppermute | solution.py:42
  176.8 4.5 %collective-permute-start.15 = (f32[512,512]{1,0:T(8,128)S(1)}, f32[512,512]{1,0:T(8,128)S(1)}, u32[]{:S(2)}, u32[]{:S(2)}) collective-permute-start(f32[512,512]{1,0:T(8,128)S(1)} %get-tuple-element.18), channel_id=1, source_target_pairs={{0,1},{1,0},{2,3},{3,2},{4,5},{5,4},{6,7},{7,6},{8,9},{9,8},{10,11... | collective-permute-start | bytes 3145736 | tf_op jit(solution)/shard_map/ppermute | solution.py:42
  182.3 22.0 %all-to-all-start.2 = ((bf16[16,32,512]{2,1,0:T(8,128)(2,1)}), bf16[16,32,512]{2,1,0:T(8,128)(2,1)S(1)}, u32[]{:S(2)}, u32[]{:S(2)}) async-start(bf16[16,32,512]{2,1,0:T(8,128)(2,1)} %bitcast.6), calls=%async_computation.2 | async-start | bytes 1048576 | tf_op jit(solution)/shard_map/all_to_all | solution.py:253
  185.9 2.9 %copy-start.7 = (bf16[1024,1536]{1,0:T(8,128)(2,1)S(1)}, bf16[1024,1536]{1,0:T(8,128)(2,1)}, u32[]{:S(2)}) copy-start(bf16[1024,1536]{1,0:T(8,128)(2,1)} %copy-done.6) | copy-start | bytes 9437188
  (2 other events, 2.8 us)

commit v4 on v3

--- a/solution.py
+++ b/solution.py
@@ -92,18 +92,19 @@
             trio[:, at : at + LANES] = value
 
 
-def backward_kernel(zh_size, gate_w, up_w, trio_in, *refs):
+def order_blocks(zh_size, refs, trio, arrived, skip=0):
     size = 2 * zh_size
-    rights, refs = refs[:zh_size], refs[zh_size:]
-    lefts, refs = refs[: zh_size - 1], refs[zh_size - 1 :]
-    beside, (trio_out, in_own, in_other, trio, arrived, left) = refs[:zh_size], refs[zh_size:]
-    rows, ff = trio_in.shape[0], gate_w.shape[1]
+    trio_in, rights, refs = refs[0], refs[1 : 1 + zh_size], refs[1 + zh_size :]
+    lefts, beside = refs[: zh_size - 1], refs[zh_size - 1 :]
+    rows = trio_in.shape[0]
     z, xh = 2 * lax.axis_index("zh") + lax.axis_index("zl"), lax.axis_index("xh")
     copies = []
 
     def put(distance, mine, others):
         block = 2 * rows * lax.rem(z + distance + size, size)
         for source, half in ((mine, xh), (others, 1 - xh)):
+            if skip:
+                source = source.at[:, pl.ds(skip, source.shape[1] - skip)]
             at = pl.multiple_of(block + rows * half, rows)
             copies.append(
                 pltpu.make_async_copy(
@@ -121,15 +122,29 @@
     put(-zh_size, rights[-1], beside[-1])
     for copy in copies:
         copy.wait()
-    copy = pltpu.make_async_copy(trio, trio_out, left)
-    copy.start()
-    share = in_own.shape[0]
+
+
+def input_kernel(zh_size, gate_w, up_w, *refs):
+    blocks_in, (in_own, in_other, duo, arrived) = refs[:-4], refs[-4:]
+    share, ff = in_own.shape[0], gate_w.shape[1]
+    order_blocks(zh_size, blocks_in, duo, arrived, ff)
     for part, target in ((1, in_other), (0, in_own)):
         at = slice(part * share, (part + 1) * share)
-        target[...] = contract_cols(trio[at, ff : 2 * ff], gate_w[...]) + contract_cols(
-            trio[at, 2 * ff :], up_w[...]
+        target[...] = contract_cols(duo[at, :ff], gate_w[...]) + contract_cols(
+            duo[at, ff:], up_w[...]
         )
-    copy.wait()
+
+
+def weight_kernel(zh_size, own, other, *refs):
+    blocks_in, (gate_wgrad, up_wgrad, down_wgrad, trio, arrived) = refs[:-5], refs[-5:]
+    order_blocks(zh_size, blocks_in, trio, arrived)
+    depth, ff = gate_wgrad.shape
+    every = [x[...].reshape(-1, 2 * depth) for x in (own, other)]
+    every = jnp.concatenate(every, axis=0)
+    inputs, grads = every[:, :depth], every[:, depth:]
+    down_wgrad[...] = contract_rows(trio[:, :ff], grads).astype(jnp.bfloat16)
+    gate_wgrad[...] = contract_rows(inputs, trio[:, ff : 2 * ff]).astype(jnp.bfloat16)
+    up_wgrad[...] = contract_rows(inputs, trio[:, 2 * ff :]).astype(jnp.bfloat16)
 
 
 def pair_swap(x, zh_size):
@@ -223,41 +238,48 @@
 
     blocks_in = [trio] + right[1:] + left[1:] + beside
     share = half_tokens
-    trio, in_own, in_other = pl.pallas_call(
-        functools.partial(backward_kernel, zh_size),
-        out_shape=(
-            jax.ShapeDtypeStruct((2 * share, 3 * ff), jnp.bfloat16),
-            jax.ShapeDtypeStruct((share, depth), jnp.float32),
-            jax.ShapeDtypeStruct((share, depth), jnp.float32),
-        ),
-        in_specs=[pl.BlockSpec(memory_space=pltpu.VMEM)] * 2
-        + [pl.BlockSpec(memory_space=pltpu.HBM)] * len(blocks_in),
-        out_specs=[pl.BlockSpec(memory_space=pltpu.HBM)]
-        + [pl.BlockSpec(memory_space=pltpu.VMEM)] * 2,
-        scratch_shapes=[
-            pltpu.VMEM((2 * share, 3 * ff), jnp.bfloat16),
+    vmem, hbm = pl.BlockSpec(memory_space=pltpu.VMEM), pl.BlockSpec(memory_space=pltpu.HBM)
+
+    def ordering(width):
+        return [
+            pltpu.VMEM((2 * share, width), jnp.bfloat16),
             pltpu.SemaphoreType.DMA((4 * zh_size,)),
-            pltpu.SemaphoreType.DMA,
-        ],
+        ]
+
+    in_own, in_other = pl.pallas_call(
+        functools.partial(input_kernel, zh_size),
+        out_shape=[jax.ShapeDtypeStruct((share, depth), jnp.float32)] * 2,
+        in_specs=[vmem] * 2 + [hbm] * len(blocks_in),
+        out_specs=[vmem] * 2,
+        scratch_shapes=ordering(2 * ff),
         compiler_params=pltpu.CompilerParams(vmem_limit_bytes=40 * 2**20),
         cost_estimate=pl.CostEstimate(
             flops=8 * share * depth * ff, bytes_accessed=9 * 2**20, transcendentals=0
         ),
         name="input_gradient",
     )(gate_weight, up_weight, *blocks_in)
-    hidden, gate_grad, up_grad = trio[:, :ff], trio[:, ff : 2 * ff], trio[:, 2 * ff :]
-
-    every = jnp.concatenate([x.reshape(-1, 2 * depth) for x in (own, other)], axis=0)
-    inputs, grads = every[:, :depth], every[:, depth:]
     in_part = in_own + swap(in_other, "c")
     in_part = lax.all_to_all(
         in_part.astype(jnp.bfloat16).reshape(blocks, rows, depth), ("y", "xl"), 0, 0, tiled=True
     )
     in_grad = jnp.sum(in_part.astype(jnp.float32), axis=0).astype(jnp.bfloat16)
 
-    down_wgrad = contract_rows(hidden, grads).astype(jnp.bfloat16)
-    gate_wgrad = contract_rows(inputs, gate_grad).astype(jnp.bfloat16)
-    up_wgrad = contract_rows(inputs, up_grad).astype(jnp.bfloat16)
+    gate_wgrad, up_wgrad, down_wgrad = pl.pallas_call(
+        functools.partial(weight_kernel, zh_size),
+        out_shape=[
+            jax.ShapeDtypeStruct((depth, ff), jnp.bfloat16),
+            jax.ShapeDtypeStruct((depth, ff), jnp.bfloat16),
+            jax.ShapeDtypeStruct((ff, depth), jnp.bfloat16),
+        ],
+        in_specs=[vmem] * 2 + [hbm] * len(blocks_in),
+        out_specs=[vmem] * 3,
+        scratch_shapes=ordering(3 * ff),
+        compiler_params=pltpu.CompilerParams(vmem_limit_bytes=40 * 2**20),
+        cost_estimate=pl.CostEstimate(
+            flops=12 * share * depth * ff, bytes_accessed=9 * 2**20, transcendentals=0
+        ),
+        name="weight_gradients",
+    )(own, other, *blocks_in)
     return (in_grad, gate_wgrad, up_wgrad, down_wgrad)
 
 

time: 206 us -> 202 us (0.981)
  waiting for transfers between devices: 72.2 us -> 66.2 us
  matrix products: 5.97 us -> 0 us
  local copies, waits for them, and re-layouts: 3.93 us -> 7.25 us
  Pallas kernels: 8.13 us -> 11.2 us
    dot_general x3 -> x0, matrix products: 5.97 us -> none  [contract_rows(): lax.dot_general(left, right, (((0,), (0,)), ((), ())), preferred_element_...]
    all_to_all x1, waiting for transfers between devices: 12.5 us -> 6.51 us  [per_device(): lax.all_to_all(in_part.astype(jnp.bfloat16).reshape(blocks, rows, depth),...]
    unnamed x16 -> x52, local copies, waits for them, and re-layouts: 2.83 us -> 6.15 us
    pallas_call x1 -> x2, Pallas kernels: 5.79 us -> 8.87 us  [the longest x1 7.02 us: per_device(): pl.pallas_call(functools.partial(weight_kernel, zh_size), out_shape=[jax....]
  transfers between devices with their start and end apart: 18 -> 18, of which waited for: 12 -> 12; matrix products, arithmetic and copies ran while one was open for 3% -> 0% of each run, Pallas kernels for 0% -> 3%
where the time goes in v4:
time: 202 us; the launch traced here: 201 us
  waiting for transfers between devices  66.2 us (33%)
  starting transfers between devices  58.5 us (29%)
  blocking collectives  52.8 us (26%)
  Pallas kernels  11.2 us (6%)
  local copies, waits for them, and re-layouts  7.25 us (4%)
  other arithmetic  4.23 us (2%)
    all_to_all x1, blocking collectives, per_device(): lax.all_to_all(parts.astype(jnp.float16), ('zh', 'xh'), 0, 0, tiled=True)  52.8 us
    ppermute x3, waiting for transfers between devices, pair_swap(): return lax.ppermute(x, ('zh', 'zl', 'c'), pairs)  29.1 us
    ppermute x7, starting transfers between devices, turn(): lax.ppermute(x, ('zh', 'zl'), [(i, (i + step) % size) for i in range(size)])  19.4 us
    ppermute x6, starting transfers between devices, swap(): return lax.ppermute(x, axis, [(0, 1), (1, 0)])  16.7 us
    ppermute x7, waiting for transfers between devices, turn(): lax.ppermute(x, ('zh', 'zl'), [(i, (i + step) % size) for i in range(size)])  16.1 us
    ppermute x3, starting transfers between devices, pair_swap(): return lax.ppermute(x, ('zh', 'zl', 'c'), pairs)  10.3 us
    ppermute x6, waiting for transfers between devices, swap(): return lax.ppermute(x, axis, [(0, 1), (1, 0)])  9.72 us
    all_to_all x1, starting transfers between devices, per_device(): lax.all_to_all(jnp.broadcast_to(shard[None], (blocks, rows, 2 * depth)),...  7.84 us
  transfers between devices with their start and end apart: 18, of which 12 were waited for; matrix products, arithmetic and copies ran while one was open for 0% of the time, Pallas kernels for 3%

profile of v4, /device:TPU:4, one launch (start us, length us, event | category | flops | bytes accessed | tf_op | source)
XLA Modules:
  0.0 201.3 jit_solution(9885658545974059627)
XLA Ops:
  2.5 7.8 %all-to-all-start = ((bf16[16,32,1024]{2,1,0:T(8,128)(2,1)}), bf16[16,32,1024]{2,1,0:T(8,128)(2,1)S(1)}, u32[]{:S(2)}, u32[]{:S(2)}) async-start(bf16[16,32,1024]{2,1,0:T(8,128)(2,1)} %broadcast_in_dim.10), calls=%async_computation | async-start | bytes 2097152 | tf_op jit(solution)/shard_map/all_to_all | solution.py:179
  10.5 4.3 %collective-permute-start = (bf16[1536,512]{1,0:T(8,128)(2,1)S(1)}, bf16[1536,512]{1,0:T(8,128)(2,1)S(1)}, u32[]{:S(2)}, u32[]{:S(2)}) collective-permute-start(bf16[1536,512]{1,0:T(8,128)(2,1)S(1)} %pad_maximum_fusion), channel_id=1, source_target_pairs={{0,64},{1,449},{64,0},{65,129},{128,192},{129,65},{192,128},{193,2... | collective-permute-start | bytes 4718600 | tf_op jit(solution)/shard_map/ppermute | solution.py:157
  14.8 18.4 %collective-permute-done.far = bf16[1536,512]{1,0:T(8,128)(2,1)S(1)} collective-permute-done((bf16[1536,512]{1,0:T(8,128)(2,1)S(1)}, bf16[1536,512]{1,0:T(8,128)(2,1)S(1)}, u32[]{:S(2)}, u32[]{:S(2)}) %collective-permute-start) | collective-permute-done | bytes 1572896 | tf_op jit(solution)/shard_map/ppermute | solution.py:157
  34.4 4.7 %all-to-all-done = bf16[16,32,1024]{2,1,0:T(8,128)(2,1)S(1)} async-done(((bf16[16,32,1024]{2,1,0:T(8,128)(2,1)}), bf16[16,32,1024]{2,1,0:T(8,128)(2,1)S(1)}, u32[]{:S(2)}, u32[]{:S(2)}) %all-to-all-start) | async-done | bytes 1048608 | tf_op jit(solution)/shard_map/all_to_all | solution.py:179
  39.1 2.9 %collective-permute-start.1 = (bf16[2,2,128,1024]{3,2,1,0:T(8,128)(2,1)S(1)}, bf16[2,2,128,1024]{3,2,1,0:T(8,128)(2,1)S(1)}, u32[]{:S(2)}, u32[]{:S(2)}) collective-permute-start(bf16[2,2,128,1024]{3,2,1,0:T(8,128)(2,1)S(1)} %bitcast.9), channel_id=1, source_target_pairs={{0,1},{1,0},{2,3},{3,2},{4,5},{5,4},{6,7},{7,6},{8,9},{9,8},{10,11... | collective-permute-start | bytes 3145736 | tf_op jit(solution)/shard_map/ppermute | solution.py:42
  42.0 3.5 %collective-permute-start.2 = (bf16[2,128,1024]{2,1,0:T(8,128)(2,1)S(1)}, bf16[2,128,1024]{2,1,0:T(8,128)(2,1)S(1)}, u32[]{:S(2)}, u32[]{:S(2)}) collective-permute-start(bf16[2,128,1024]{2,1,0:T(8,128)(2,1)S(1)} %fusion.1), channel_id=1, source_target_pairs={{0,64},{1,449},{64,0},{65,129},{128,192},{129,65},{192,128},{193,2... | collective-permute-start | bytes 1572872 | tf_op jit(solution)/shard_map/ppermute | solution.py:157
  45.6 2.5 %collective-permute-start.3 = (bf16[2,128,1024]{2,1,0:T(8,128)(2,1)S(1)}, bf16[2,128,1024]{2,1,0:T(8,128)(2,1)S(1)}, u32[]{:S(2)}, u32[]{:S(2)}) collective-permute-start(bf16[2,128,1024]{2,1,0:T(8,128)(2,1)S(1)} %fusion), channel_id=1, source_target_pairs={{0,64},{1,449},{64,0},{65,129},{128,192},{129,65},{192,128},{193,2... | collective-permute-start | bytes 1572872 | tf_op jit(solution)/shard_map/ppermute | solution.py:157
  48.1 5.1 %collective-permute-done.2 = bf16[2,128,1024]{2,1,0:T(8,128)(2,1)S(1)} collective-permute-done((bf16[2,128,1024]{2,1,0:T(8,128)(2,1)S(1)}, bf16[2,128,1024]{2,1,0:T(8,128)(2,1)S(1)}, u32[]{:S(2)}, u32[]{:S(2)}) %collective-permute-start.2) | collective-permute-done | bytes 524320 | tf_op jit(solution)/shard_map/ppermute | solution.py:157
  53.2 5.6 %collective-permute-done.3 = bf16[2,128,1024]{2,1,0:T(8,128)(2,1)S(1)} collective-permute-done((bf16[2,128,1024]{2,1,0:T(8,128)(2,1)S(1)}, bf16[2,128,1024]{2,1,0:T(8,128)(2,1)S(1)}, u32[]{:S(2)}, u32[]{:S(2)}) %collective-permute-start.3) | collective-permute-done | bytes 524320 | tf_op jit(solution)/shard_map/ppermute | solution.py:157
  61.1 52.8 %all_to_all.15 = f16[8,784,128]{2,1,0:T(8,128)(2,1)S(1)} all-to-all(f16[8,784,128]{2,1,0:T(8,128)(2,1)S(1)} %convert_element_type.11), channel_id=1, replica_groups=mesh['zh'=4,'zl'=2,'xh'=2,'y'=8,'xl'=2,'c'=2] {'zh','xh'}, dimensions={0} | all-to-all | bytes 3211264 | tf_op jit(solution)/shard_map/all_to_all | solution.py:208
  114.4 2.6 %collective-permute-start.7 = (bf16[64,1536]{1,0:T(8,128)(2,1)S(1)}, bf16[64,1536]{1,0:T(8,128)(2,1)S(1)}, u32[]{:S(2)}, u32[]{:S(2)}) collective-permute-start(bf16[64,1536]{1,0:T(8,128)(2,1)S(1)} %hidden_and_grads.1.refs_0_), channel_id=1, source_target_pairs={{0,448},{64,0},{128,64},{192,128},{256,192},{320,256},{384,320},{4... | collective-permute-start | bytes 589832 | tf_op jit(solution)/shard_map/ppermute | solution.py:161
  117.0 3.3 %collective-permute-start.4 = (bf16[64,1536]{1,0:T(8,128)(2,1)S(1)}, bf16[64,1536]{1,0:T(8,128)(2,1)S(1)}, u32[]{:S(2)}, u32[]{:S(2)}) collective-permute-start(bf16[64,1536]{1,0:T(8,128)(2,1)S(1)} %hidden_and_grads.1.refs_0_), channel_id=1, source_target_pairs={{0,64},{64,128},{128,192},{192,256},{256,320},{320,384},{384,448},... | collective-permute-start | bytes 589832 | tf_op jit(solution)/shard_map/ppermute | solution.py:161
  122.0 4.5 %collective-permute-done.4.refs_1_ = bf16[64,1536]{1,0:T(8,128)(2,1)S(1)} collective-permute-done((bf16[64,1536]{1,0:T(8,128)(2,1)S(1)}, bf16[64,1536]{1,0:T(8,128)(2,1)S(1)}, u32[]{:S(2)}, u32[]{:S(2)}) %collective-permute-start.4) | collective-permute-done | bytes 196640 | tf_op jit(solution)/shard_map/ppermute | solution.py:161
  126.5 5.1 %collective-permute-start.10 = (bf16[192,1536]{1,0:T(8,128)(2,1)S(1)}, bf16[192,1536]{1,0:T(8,128)(2,1)S(1)}, u32[]{:S(2)}, u32[]{:S(2)}) collective-permute-start(bf16[192,1536]{1,0:T(8,128)(2,1)S(1)} %pad_maximum_fusion.1), channel_id=1, source_target_pairs={{0,32},{32,0},{1,33},{33,1},{2,34},{34,2},{3,35},{35,3},{4,36},{36... | collective-permute-start | bytes 1769480 | tf_op jit(solution)/shard_map/ppermute | solution.py:42
  133.5 3.9 %collective-permute-start.5 = (bf16[64,1536]{1,0:T(8,128)(2,1)S(1)}, bf16[64,1536]{1,0:T(8,128)(2,1)S(1)}, u32[]{:S(2)}, u32[]{:S(2)}) collective-permute-start(bf16[64,1536]{1,0:T(8,128)(2,1)S(1)} %collective-permute-done.4.refs_1_), channel_id=1, source_target_pairs={{0,64},{64,128},{128,192},{192,256},{256,320},{320,384},{384,448},... | collective-permute-start | bytes 589832 | tf_op jit(solution)/shard_map/ppermute | solution.py:161
  139.2 3.1 %collective-permute-start.9 = (bf16[64,1536]{1,0:T(8,128)(2,1)S(1)}, bf16[64,1536]{1,0:T(8,128)(2,1)S(1)}, u32[]{:S(2)}, u32[]{:S(2)}) collective-permute-start(bf16[64,1536]{1,0:T(8,128)(2,1)S(1)} %collective-permute-done.8.refs_6_), channel_id=1, source_target_pairs={{0,448},{64,0},{128,64},{192,128},{256,192},{320,256},{384,320},{4... | collective-permute-start | bytes 589832 | tf_op jit(solution)/shard_map/ppermute | solution.py:161
  142.3 2.7 %collective-permute-start.6 = (bf16[64,1536]{1,0:T(8,128)(2,1)S(1)}, bf16[64,1536]{1,0:T(8,128)(2,1)S(1)}, u32[]{:S(2)}, u32[]{:S(2)}) collective-permute-start(bf16[64,1536]{1,0:T(8,128)(2,1)S(1)} %collective-permute-done.5.refs_2_), channel_id=1, source_target_pairs={{0,64},{64,128},{128,192},{192,256},{256,320},{320,384},{384,448},... | collective-permute-start | bytes 589832 | tf_op jit(solution)/shard_map/ppermute | solution.py:161
  147.4 3.7 %collective-permute-done.6.refs_3_ = bf16[64,1536]{1,0:T(8,128)(2,1)S(1)} collective-permute-done((bf16[64,1536]{1,0:T(8,128)(2,1)S(1)}, bf16[64,1536]{1,0:T(8,128)(2,1)S(1)}, u32[]{:S(2)}, u32[]{:S(2)}) %collective-permute-start.6) | collective-permute-done | bytes 196640 | tf_op jit(solution)/shard_map/ppermute | solution.py:161
  155.3 4.5 %collective-permute-done.11.refs_4_ = bf16[64,1536]{1,0:T(8,128)(2,1)S(1)} collective-permute-done((bf16[64,1536]{1,0:T(8,128)(2,1)S(1)}, bf16[64,1536]{1,0:T(8,128)(2,1)S(1)}, u32[]{:S(2)}, u32[]{:S(2)}) %collective-permute-start.11) | collective-permute-done | bytes 196640 | tf_op jit(solution)/shard_map/ppermute | solution.py:161
  162.2 7.1 %collective-permute-done.14.refs_11_ = bf16[64,1536]{1,0:T(8,128)(2,1)S(1)} collective-permute-done((bf16[64,1536]{1,0:T(8,128)(2,1)S(1)}, bf16[64,1536]{1,0:T(8,128)(2,1)S(1)}, u32[]{:S(2)}, u32[]{:S(2)}) %collective-permute-start.14) | collective-permute-done | bytes 196640 | tf_op jit(solution)/shard_map/ppermute | solution.py:42
  173.1 2.6 %collective-permute-done.15 = f32[512,512]{1,0:T(8,128)S(1)} collective-permute-done((f32[512,512]{1,0:T(8,128)S(1)}, f32[512,512]{1,0:T(8,128)S(1)}, u32[]{:S(2)}, u32[]{:S(2)}) %collective-permute-start.15) | collective-permute-done | bytes 1048608 | tf_op jit(solution)/shard_map/ppermute | solution.py:42
  176.8 4.2 %all-to-all-start.2 = ((bf16[16,32,512]{2,1,0:T(8,128)(2,1)}), bf16[16,32,512]{2,1,0:T(8,128)(2,1)}, u32[]{:S(2)}, u32[]{:S(2)}) async-start(bf16[16,32,512]{2,1,0:T(8,128)(2,1)} %bitcast.15), calls=%async_computation.2 | async-start | bytes 1048576 | tf_op jit(solution)/shard_map/all_to_all | solution.py:262
  186.0 7.0 %weight_gradients.1 = (bf16[512,512]{1,0:T(8,128)(2,1)}, bf16[512,512]{1,0:T(8,128)(2,1)}, bf16[512,512]{1,0:T(8,128)(2,1)}) custom-call(bf16[2,2,128,1024]{3,2,1,0:T(8,128)(2,1)S(1)} %bitcast.12, bf16[2,2,128,1024]{3,2,1,0:T(8,128)(2,1)S(1)} %collective-permute-done.1.other, bf16[64,1536]{1,0:T(8,128)(2,1)S(1)} %hidden_and_grads.1.refs_0_, ...), custom_call_target="tpu_custom_call" | custom-call | flops 1610612736 | bytes 9437184 | tf_op jit(solution)/shard_map/weight_gradients/pallas_call | solution.py:267
  193.0 6.5 %all-to-all-done.2 = bf16[16,32,512]{2,1,0:T(8,128)(2,1)} async-done(((bf16[16,32,512]{2,1,0:T(8,128)(2,1)}), bf16[16,32,512]{2,1,0:T(8,128)(2,1)}, u32[]{:S(2)}, u32[]{:S(2)}) %all-to-all-start.2) | async-done | bytes 524320 | tf_op jit(solution)/shard_map/all_to_all | solution.py:262
  (81 shorter events, 31.7 us)
Async XLA Ops:
  2.5 36.5 %all-to-all-start = ((bf16[16,32,1024]{2,1,0:T(8,128)(2,1)}), bf16[16,32,1024]{2,1,0:T(8,128)(2,1)S(1)}, u32[]{:S(2)}, u32[]{:S(2)}) async-start(bf16[16,32,1024]{2,1,0:T(8,128)(2,1)} %broadcast_in_dim.10), calls=%async_computation | async-start | bytes 2097152 | tf_op jit(solution)/shard_map/all_to_all | solution.py:179
  10.5 22.7 %collective-permute-start = (bf16[1536,512]{1,0:T(8,128)(2,1)S(1)}, bf16[1536,512]{1,0:T(8,128)(2,1)S(1)}, u32[]{:S(2)}, u32[]{:S(2)}) collective-permute-start(bf16[1536,512]{1,0:T(8,128)(2,1)S(1)} %pad_maximum_fusion), channel_id=1, source_target_pairs={{0,64},{1,449},{64,0},{65,129},{128,192},{129,65},{192,128},{193,2... | collective-permute-start | bytes 4718600 | tf_op jit(solution)/shard_map/ppermute | solution.py:157
  39.1 6.4 %collective-permute-start.1 = (bf16[2,2,128,1024]{3,2,1,0:T(8,128)(2,1)S(1)}, bf16[2,2,128,1024]{3,2,1,0:T(8,128)(2,1)S(1)}, u32[]{:S(2)}, u32[]{:S(2)}) collective-permute-start(bf16[2,2,128,1024]{3,2,1,0:T(8,128)(2,1)S(1)} %bitcast.9), channel_id=1, source_target_pairs={{0,1},{1,0},{2,3},{3,2},{4,5},{5,4},{6,7},{7,6},{8,9},{9,8},{10,11... | collective-permute-start | bytes 3145736 | tf_op jit(solution)/shard_map/ppermute | solution.py:42
  42.0 11.2 %collective-permute-start.2 = (bf16[2,128,1024]{2,1,0:T(8,128)(2,1)S(1)}, bf16[2,128,1024]{2,1,0:T(8,128)(2,1)S(1)}, u32[]{:S(2)}, u32[]{:S(2)}) collective-permute-start(bf16[2,128,1024]{2,1,0:T(8,128)(2,1)S(1)} %fusion.1), channel_id=1, source_target_pairs={{0,64},{1,449},{64,0},{65,129},{128,192},{129,65},{192,128},{193,2... | collective-permute-start | bytes 1572872 | tf_op jit(solution)/shard_map/ppermute | solution.py:157
  45.6 13.3 %collective-permute-start.3 = (bf16[2,128,1024]{2,1,0:T(8,128)(2,1)S(1)}, bf16[2,128,1024]{2,1,0:T(8,128)(2,1)S(1)}, u32[]{:S(2)}, u32[]{:S(2)}) collective-permute-start(bf16[2,128,1024]{2,1,0:T(8,128)(2,1)S(1)} %fusion), channel_id=1, source_target_pairs={{0,64},{1,449},{64,0},{65,129},{128,192},{129,65},{192,128},{193,2... | collective-permute-start | bytes 1572872 | tf_op jit(solution)/shard_map/ppermute | solution.py:157
  114.4 7.6 %collective-permute-start.7 = (bf16[64,1536]{1,0:T(8,128)(2,1)S(1)}, bf16[64,1536]{1,0:T(8,128)(2,1)S(1)}, u32[]{:S(2)}, u32[]{:S(2)}) collective-permute-start(bf16[64,1536]{1,0:T(8,128)(2,1)S(1)} %hidden_and_grads.1.refs_0_), channel_id=1, source_target_pairs={{0,448},{64,0},{128,64},{192,128},{256,192},{320,256},{384,320},{4... | collective-permute-start | bytes 589832 | tf_op jit(solution)/shard_map/ppermute | solution.py:161
  117.0 9.5 %collective-permute-start.4 = (bf16[64,1536]{1,0:T(8,128)(2,1)S(1)}, bf16[64,1536]{1,0:T(8,128)(2,1)S(1)}, u32[]{:S(2)}, u32[]{:S(2)}) collective-permute-start(bf16[64,1536]{1,0:T(8,128)(2,1)S(1)} %hidden_and_grads.1.refs_0_), channel_id=1, source_target_pairs={{0,64},{64,128},{128,192},{192,256},{256,320},{320,384},{384,448},... | collective-permute-start | bytes 589832 | tf_op jit(solution)/shard_map/ppermute | solution.py:161
  126.5 44.6 %copy-start.6 = (bf16[64,1536]{1,0:T(8,128)(2,1)}, bf16[64,1536]{1,0:T(8,128)(2,1)S(1)}, u32[]{:S(2)}) copy-start(bf16[64,1536]{1,0:T(8,128)(2,1)S(1)} %collective-permute-done.4.refs_1_) | copy-start | bytes 589828
  126.5 24.6 %collective-permute-start.10 = (bf16[192,1536]{1,0:T(8,128)(2,1)S(1)}, bf16[192,1536]{1,0:T(8,128)(2,1)S(1)}, u32[]{:S(2)}, u32[]{:S(2)}) collective-permute-start(bf16[192,1536]{1,0:T(8,128)(2,1)S(1)} %pad_maximum_fusion.1), channel_id=1, source_target_pairs={{0,32},{32,0},{1,33},{33,1},{2,34},{34,2},{3,35},{35,3},{4,36},{36... | collective-permute-start | bytes 1769480 | tf_op jit(solution)/shard_map/ppermute | solution.py:42
  131.6 7.6 %collective-permute-start.8 = (bf16[64,1536]{1,0:T(8,128)(2,1)S(1)}, bf16[64,1536]{1,0:T(8,128)(2,1)S(1)}, u32[]{:S(2)}, u32[]{:S(2)}) collective-permute-start(bf16[64,1536]{1,0:T(8,128)(2,1)S(1)} %collective-permute-done.7.refs_5_), channel_id=1, source_target_pairs={{0,448},{64,0},{128,64},{192,128},{256,192},{320,256},{384,320},{4... | collective-permute-start | bytes 589832 | tf_op jit(solution)/shard_map/ppermute | solution.py:161
  133.5 8.8 %collective-permute-start.5 = (bf16[64,1536]{1,0:T(8,128)(2,1)S(1)}, bf16[64,1536]{1,0:T(8,128)(2,1)S(1)}, u32[]{:S(2)}, u32[]{:S(2)}) collective-permute-start(bf16[64,1536]{1,0:T(8,128)(2,1)S(1)} %collective-permute-done.4.refs_1_), channel_id=1, source_target_pairs={{0,64},{64,128},{128,192},{192,256},{256,320},{320,384},{384,448},... | collective-permute-start | bytes 589832 | tf_op jit(solution)/shard_map/ppermute | solution.py:161
  139.2 32.0 %copy-start.8 = (bf16[64,1536]{1,0:T(8,128)(2,1)}, bf16[64,1536]{1,0:T(8,128)(2,1)S(1)}, u32[]{:S(2)}) copy-start(bf16[64,1536]{1,0:T(8,128)(2,1)S(1)} %collective-permute-done.8.refs_6_) | copy-start | bytes 589828
  139.2 8.2 %collective-permute-start.9 = (bf16[64,1536]{1,0:T(8,128)(2,1)S(1)}, bf16[64,1536]{1,0:T(8,128)(2,1)S(1)}, u32[]{:S(2)}, u32[]{:S(2)}) collective-permute-start(bf16[64,1536]{1,0:T(8,128)(2,1)S(1)} %collective-permute-done.8.refs_6_), channel_id=1, source_target_pairs={{0,448},{64,0},{128,64},{192,128},{256,192},{320,256},{384,320},{4... | collective-permute-start | bytes 589832 | tf_op jit(solution)/shard_map/ppermute | solution.py:161
  142.3 28.8 %copy-start.10 = (bf16[64,1536]{1,0:T(8,128)(2,1)}, bf16[64,1536]{1,0:T(8,128)(2,1)S(1)}, u32[]{:S(2)}) copy-start(bf16[64,1536]{1,0:T(8,128)(2,1)S(1)} %collective-permute-done.5.refs_2_) | copy-start | bytes 589828
  142.3 8.8 %collective-permute-start.6 = (bf16[64,1536]{1,0:T(8,128)(2,1)S(1)}, bf16[64,1536]{1,0:T(8,128)(2,1)S(1)}, u32[]{:S(2)}, u32[]{:S(2)}) collective-permute-start(bf16[64,1536]{1,0:T(8,128)(2,1)S(1)} %collective-permute-done.5.refs_2_), channel_id=1, source_target_pairs={{0,64},{64,128},{128,192},{192,256},{256,320},{320,384},{384,448},... | collective-permute-start | bytes 589832 | tf_op jit(solution)/shard_map/ppermute | solution.py:161
  145.1 17.1 %collective-permute-start.12 = (bf16[128,1536]{1,0:T(8,128)(2,1)S(1)}, bf16[128,1536]{1,0:T(8,128)(2,1)S(1)}, u32[]{:S(2)}, u32[]{:S(2)}) collective-permute-start(bf16[128,1536]{1,0:T(8,128)(2,1)S(1)} %pad_maximum_fusion.2), channel_id=1, source_target_pairs={{0,32},{32,0},{1,33},{33,1},{2,34},{34,2},{3,35},{35,3},{4,36},{36... | collective-permute-start | bytes 1179656 | tf_op jit(solution)/shard_map/ppermute | solution.py:42
  147.4 23.8 %copy-start.12 = (bf16[64,1536]{1,0:T(8,128)(2,1)}, bf16[64,1536]{1,0:T(8,128)(2,1)S(1)}, u32[]{:S(2)}) copy-start(bf16[64,1536]{1,0:T(8,128)(2,1)S(1)} %collective-permute-done.9.refs_7_) | copy-start | bytes 589828
  151.1 20.1 %copy-start.14 = (bf16[64,1536]{1,0:T(8,128)(2,1)}, bf16[64,1536]{1,0:T(8,128)(2,1)S(1)}, u32[]{:S(2)}) copy-start(bf16[64,1536]{1,0:T(8,128)(2,1)S(1)} %collective-permute-done.6.refs_3_) | copy-start | bytes 589828
  151.1 20.1 %copy-start.16 = (bf16[192,1536]{1,0:T(8,128)(2,1)}, bf16[192,1536]{1,0:T(8,128)(2,1)S(1)}, u32[]{:S(2)}) copy-start(bf16[192,1536]{1,0:T(8,128)(2,1)S(1)} %collective-permute-done.10.refs_8_) | copy-start | bytes 1769476
  151.1 8.8 %collective-permute-start.11 = (bf16[64,1536]{1,0:T(8,128)(2,1)S(1)}, bf16[64,1536]{1,0:T(8,128)(2,1)S(1)}, u32[]{:S(2)}, u32[]{:S(2)}) collective-permute-start(bf16[64,1536]{1,0:T(8,128)(2,1)S(1)} %collective-permute-done.6.refs_3_), channel_id=1, source_target_pairs={{0,64},{64,128},{128,192},{192,256},{256,320},{320,384},{384,448},... | collective-permute-start | bytes 589832 | tf_op jit(solution)/shard_map/ppermute | solution.py:161
  153.0 16.2 %collective-permute-start.13 = (bf16[128,1536]{1,0:T(8,128)(2,1)S(1)}, bf16[128,1536]{1,0:T(8,128)(2,1)S(1)}, u32[]{:S(2)}, u32[]{:S(2)}) collective-permute-start(bf16[128,1536]{1,0:T(8,128)(2,1)S(1)} %pad_maximum_fusion.3), channel_id=1, source_target_pairs={{0,32},{32,0},{1,33},{33,1},{2,34},{34,2},{3,35},{35,3},{4,36},{36... | collective-permute-start | bytes 1179656 | tf_op jit(solution)/shard_map/ppermute | solution.py:42
  159.9 9.4 %collective-permute-start.14 = (bf16[64,1536]{1,0:T(8,128)(2,1)S(1)}, bf16[64,1536]{1,0:T(8,128)(2,1)S(1)}, u32[]{:S(2)}, u32[]{:S(2)}) collective-permute-start(bf16[64,1536]{1,0:T(8,128)(2,1)S(1)} %collective-permute-done.11.refs_4_), channel_id=1, source_target_pairs={{0,32},{32,0},{1,33},{33,1},{2,34},{34,2},{3,35},{35,3},{4,36},{36... | collective-permute-start | bytes 589832 | tf_op jit(solution)/shard_map/ppermute | solution.py:42
  171.2 4.6 %collective-permute-start.15 = (f32[512,512]{1,0:T(8,128)S(1)}, f32[512,512]{1,0:T(8,128)S(1)}, u32[]{:S(2)}, u32[]{:S(2)}) collective-permute-start(f32[512,512]{1,0:T(8,128)S(1)} %get-tuple-element.20), channel_id=1, source_target_pairs={{0,1},{1,0},{2,3},{3,2},{4,5},{5,4},{6,7},{7,6},{8,9},{9,8},{10,11... | collective-permute-start | bytes 3145736 | tf_op jit(solution)/shard_map/ppermute | solution.py:42
  176.8 22.7 %all-to-all-start.2 = ((bf16[16,32,512]{2,1,0:T(8,128)(2,1)}), bf16[16,32,512]{2,1,0:T(8,128)(2,1)}, u32[]{:S(2)}, u32[]{:S(2)}) async-start(bf16[16,32,512]{2,1,0:T(8,128)(2,1)} %bitcast.15), calls=%async_computation.2 | async-start | bytes 1048576 | tf_op jit(solution)/shard_map/all_to_all | solution.py:262
  (20 other events, 117.4 us)

commit v5 on v4

--- a/solution.py
+++ b/solution.py
@@ -130,9 +130,8 @@
     order_blocks(zh_size, blocks_in, duo, arrived, ff)
     for part, target in ((1, in_other), (0, in_own)):
         at = slice(part * share, (part + 1) * share)
-        target[...] = contract_cols(duo[at, :ff], gate_w[...]) + contract_cols(
-            duo[at, ff:], up_w[...]
-        )
+        total = contract_cols(duo[at, :ff], gate_w[...]) + contract_cols(duo[at, ff:], up_w[...])
+        target[...] = total.astype(target.dtype)
 
 
 def weight_kernel(zh_size, own, other, *refs):
@@ -248,7 +247,10 @@
 
     in_own, in_other = pl.pallas_call(
         functools.partial(input_kernel, zh_size),
-        out_shape=[jax.ShapeDtypeStruct((share, depth), jnp.float32)] * 2,
+        out_shape=[
+            jax.ShapeDtypeStruct((share, depth), jnp.float32),
+            jax.ShapeDtypeStruct((share, depth), jnp.bfloat16),
+        ],
         in_specs=[vmem] * 2 + [hbm] * len(blocks_in),
         out_specs=[vmem] * 2,
         scratch_shapes=ordering(2 * ff),

time: 202 us -> 202 us (level)
  no operation moved by 1% of the time
where the time goes in v5:
time: 202 us; the launch traced here: 201 us
  waiting for transfers between devices  65.4 us (32%)
  starting transfers between devices  58.5 us (29%)
  blocking collectives  52.8 us (26%)
  Pallas kernels  11.2 us (6%)
  local copies, waits for them, and re-layouts  7.25 us (4%)
  other arithmetic  4.24 us (2%)
    all_to_all x1, blocking collectives, per_device(): lax.all_to_all(parts.astype(jnp.float16), ('zh', 'xh'), 0, 0, tiled=True)  52.8 us
    ppermute x3, waiting for transfers between devices, pair_swap(): return lax.ppermute(x, ('zh', 'zl', 'c'), pairs)  29.1 us
    ppermute x7, starting transfers between devices, turn(): lax.ppermute(x, ('zh', 'zl'), [(i, (i + step) % size) for i in range(size)])  19.4 us
    ppermute x6, starting transfers between devices, swap(): return lax.ppermute(x, axis, [(0, 1), (1, 0)])  16.7 us
    ppermute x7, waiting for transfers between devices, turn(): lax.ppermute(x, ('zh', 'zl'), [(i, (i + step) % size) for i in range(size)])  16.1 us
    ppermute x3, starting transfers between devices, pair_swap(): return lax.ppermute(x, ('zh', 'zl', 'c'), pairs)  10.3 us
    ppermute x6, waiting for transfers between devices, swap(): return lax.ppermute(x, axis, [(0, 1), (1, 0)])  8.97 us
    all_to_all x1, starting transfers between devices, per_device(): lax.all_to_all(jnp.broadcast_to(shard[None], (blocks, rows, 2 * depth)),...  7.84 us
  transfers between devices with their start and end apart: 18, of which 12 were waited for; matrix products, arithmetic and copies ran while one was open for 0% of the time, Pallas kernels for 3%

profile of v5, /device:TPU:4, one launch (start us, length us, event | category | flops | bytes accessed | tf_op | source)
XLA Modules:
  0.0 200.5 jit_solution(3374015159745510481)
XLA Ops:
  2.5 7.8 %all-to-all-start = ((bf16[16,32,1024]{2,1,0:T(8,128)(2,1)}), bf16[16,32,1024]{2,1,0:T(8,128)(2,1)S(1)}, u32[]{:S(2)}, u32[]{:S(2)}) async-start(bf16[16,32,1024]{2,1,0:T(8,128)(2,1)} %broadcast_in_dim.10), calls=%async_computation | async-start | bytes 2097152 | tf_op jit(solution)/shard_map/all_to_all | solution.py:178
  10.5 4.3 %collective-permute-start = (bf16[1536,512]{1,0:T(8,128)(2,1)S(1)}, bf16[1536,512]{1,0:T(8,128)(2,1)S(1)}, u32[]{:S(2)}, u32[]{:S(2)}) collective-permute-start(bf16[1536,512]{1,0:T(8,128)(2,1)S(1)} %pad_maximum_fusion), channel_id=1, source_target_pairs={{0,64},{1,449},{64,0},{65,129},{128,192},{129,65},{192,128},{193,2... | collective-permute-start | bytes 4718600 | tf_op jit(solution)/shard_map/ppermute | solution.py:156
  14.8 18.4 %collective-permute-done.far = bf16[1536,512]{1,0:T(8,128)(2,1)S(1)} collective-permute-done((bf16[1536,512]{1,0:T(8,128)(2,1)S(1)}, bf16[1536,512]{1,0:T(8,128)(2,1)S(1)}, u32[]{:S(2)}, u32[]{:S(2)}) %collective-permute-start) | collective-permute-done | bytes 1572896 | tf_op jit(solution)/shard_map/ppermute | solution.py:156
  34.4 4.7 %all-to-all-done = bf16[16,32,1024]{2,1,0:T(8,128)(2,1)S(1)} async-done(((bf16[16,32,1024]{2,1,0:T(8,128)(2,1)}), bf16[16,32,1024]{2,1,0:T(8,128)(2,1)S(1)}, u32[]{:S(2)}, u32[]{:S(2)}) %all-to-all-start) | async-done | bytes 1048608 | tf_op jit(solution)/shard_map/all_to_all | solution.py:178
  39.1 2.9 %collective-permute-start.1 = (bf16[2,2,128,1024]{3,2,1,0:T(8,128)(2,1)S(1)}, bf16[2,2,128,1024]{3,2,1,0:T(8,128)(2,1)S(1)}, u32[]{:S(2)}, u32[]{:S(2)}) collective-permute-start(bf16[2,2,128,1024]{3,2,1,0:T(8,128)(2,1)S(1)} %bitcast.9), channel_id=1, source_target_pairs={{0,1},{1,0},{2,3},{3,2},{4,5},{5,4},{6,7},{7,6},{8,9},{9,8},{10,11... | collective-permute-start | bytes 3145736 | tf_op jit(solution)/shard_map/ppermute | solution.py:42
  42.0 3.5 %collective-permute-start.2 = (bf16[2,128,1024]{2,1,0:T(8,128)(2,1)S(1)}, bf16[2,128,1024]{2,1,0:T(8,128)(2,1)S(1)}, u32[]{:S(2)}, u32[]{:S(2)}) collective-permute-start(bf16[2,128,1024]{2,1,0:T(8,128)(2,1)S(1)} %fusion.1), channel_id=1, source_target_pairs={{0,64},{1,449},{64,0},{65,129},{128,192},{129,65},{192,128},{193,2... | collective-permute-start | bytes 1572872 | tf_op jit(solution)/shard_map/ppermute | solution.py:156
  45.6 2.5 %collective-permute-start.3 = (bf16[2,128,1024]{2,1,0:T(8,128)(2,1)S(1)}, bf16[2,128,1024]{2,1,0:T(8,128)(2,1)S(1)}, u32[]{:S(2)}, u32[]{:S(2)}) collective-permute-start(bf16[2,128,1024]{2,1,0:T(8,128)(2,1)S(1)} %fusion), channel_id=1, source_target_pairs={{0,64},{1,449},{64,0},{65,129},{128,192},{129,65},{192,128},{193,2... | collective-permute-start | bytes 1572872 | tf_op jit(solution)/shard_map/ppermute | solution.py:156
  48.1 5.1 %collective-permute-done.2 = bf16[2,128,1024]{2,1,0:T(8,128)(2,1)S(1)} collective-permute-done((bf16[2,128,1024]{2,1,0:T(8,128)(2,1)S(1)}, bf16[2,128,1024]{2,1,0:T(8,128)(2,1)S(1)}, u32[]{:S(2)}, u32[]{:S(2)}) %collective-permute-start.2) | collective-permute-done | bytes 524320 | tf_op jit(solution)/shard_map/ppermute | solution.py:156
  53.2 5.6 %collective-permute-done.3 = bf16[2,128,1024]{2,1,0:T(8,128)(2,1)S(1)} collective-permute-done((bf16[2,128,1024]{2,1,0:T(8,128)(2,1)S(1)}, bf16[2,128,1024]{2,1,0:T(8,128)(2,1)S(1)}, u32[]{:S(2)}, u32[]{:S(2)}) %collective-permute-start.3) | collective-permute-done | bytes 524320 | tf_op jit(solution)/shard_map/ppermute | solution.py:156
  61.1 52.8 %all_to_all.15 = f16[8,784,128]{2,1,0:T(8,128)(2,1)S(1)} all-to-all(f16[8,784,128]{2,1,0:T(8,128)(2,1)S(1)} %convert_element_type.14), channel_id=1, replica_groups=mesh['zh'=4,'zl'=2,'xh'=2,'y'=8,'xl'=2,'c'=2] {'zh','xh'}, dimensions={0} | all-to-all | bytes 3211264 | tf_op jit(solution)/shard_map/all_to_all | solution.py:207
  114.4 2.6 %collective-permute-start.7 = (bf16[64,1536]{1,0:T(8,128)(2,1)S(1)}, bf16[64,1536]{1,0:T(8,128)(2,1)S(1)}, u32[]{:S(2)}, u32[]{:S(2)}) collective-permute-start(bf16[64,1536]{1,0:T(8,128)(2,1)S(1)} %hidden_and_grads.1.refs_0_), channel_id=1, source_target_pairs={{0,448},{64,0},{128,64},{192,128},{256,192},{320,256},{384,320},{4... | collective-permute-start | bytes 589832 | tf_op jit(solution)/shard_map/ppermute | solution.py:160
  117.0 3.3 %collective-permute-start.4 = (bf16[64,1536]{1,0:T(8,128)(2,1)S(1)}, bf16[64,1536]{1,0:T(8,128)(2,1)S(1)}, u32[]{:S(2)}, u32[]{:S(2)}) collective-permute-start(bf16[64,1536]{1,0:T(8,128)(2,1)S(1)} %hidden_and_grads.1.refs_0_), channel_id=1, source_target_pairs={{0,64},{64,128},{128,192},{192,256},{256,320},{320,384},{384,448},... | collective-permute-start | bytes 589832 | tf_op jit(solution)/shard_map/ppermute | solution.py:160
  122.0 4.5 %collective-permute-done.4.refs_1_ = bf16[64,1536]{1,0:T(8,128)(2,1)S(1)} collective-permute-done((bf16[64,1536]{1,0:T(8,128)(2,1)S(1)}, bf16[64,1536]{1,0:T(8,128)(2,1)S(1)}, u32[]{:S(2)}, u32[]{:S(2)}) %collective-permute-start.4) | collective-permute-done | bytes 196640 | tf_op jit(solution)/shard_map/ppermute | solution.py:160
  126.5 5.1 %collective-permute-start.10 = (bf16[192,1536]{1,0:T(8,128)(2,1)S(1)}, bf16[192,1536]{1,0:T(8,128)(2,1)S(1)}, u32[]{:S(2)}, u32[]{:S(2)}) collective-permute-start(bf16[192,1536]{1,0:T(8,128)(2,1)S(1)} %pad_maximum_fusion.1), channel_id=1, source_target_pairs={{0,32},{32,0},{1,33},{33,1},{2,34},{34,2},{3,35},{35,3},{4,36},{36... | collective-permute-start | bytes 1769480 | tf_op jit(solution)/shard_map/ppermute | solution.py:42
  133.5 3.9 %collective-permute-start.5 = (bf16[64,1536]{1,0:T(8,128)(2,1)S(1)}, bf16[64,1536]{1,0:T(8,128)(2,1)S(1)}, u32[]{:S(2)}, u32[]{:S(2)}) collective-permute-start(bf16[64,1536]{1,0:T(8,128)(2,1)S(1)} %collective-permute-done.4.refs_1_), channel_id=1, source_target_pairs={{0,64},{64,128},{128,192},{192,256},{256,320},{320,384},{384,448},... | collective-permute-start | bytes 589832 | tf_op jit(solution)/shard_map/ppermute | solution.py:160
  139.2 3.1 %collective-permute-start.9 = (bf16[64,1536]{1,0:T(8,128)(2,1)S(1)}, bf16[64,1536]{1,0:T(8,128)(2,1)S(1)}, u32[]{:S(2)}, u32[]{:S(2)}) collective-permute-start(bf16[64,1536]{1,0:T(8,128)(2,1)S(1)} %collective-permute-done.8.refs_6_), channel_id=1, source_target_pairs={{0,448},{64,0},{128,64},{192,128},{256,192},{320,256},{384,320},{4... | collective-permute-start | bytes 589832 | tf_op jit(solution)/shard_map/ppermute | solution.py:160
  142.3 2.7 %collective-permute-start.6 = (bf16[64,1536]{1,0:T(8,128)(2,1)S(1)}, bf16[64,1536]{1,0:T(8,128)(2,1)S(1)}, u32[]{:S(2)}, u32[]{:S(2)}) collective-permute-start(bf16[64,1536]{1,0:T(8,128)(2,1)S(1)} %collective-permute-done.5.refs_2_), channel_id=1, source_target_pairs={{0,64},{64,128},{128,192},{192,256},{256,320},{320,384},{384,448},... | collective-permute-start | bytes 589832 | tf_op jit(solution)/shard_map/ppermute | solution.py:160
  147.4 3.7 %collective-permute-done.6.refs_3_ = bf16[64,1536]{1,0:T(8,128)(2,1)S(1)} collective-permute-done((bf16[64,1536]{1,0:T(8,128)(2,1)S(1)}, bf16[64,1536]{1,0:T(8,128)(2,1)S(1)}, u32[]{:S(2)}, u32[]{:S(2)}) %collective-permute-start.6) | collective-permute-done | bytes 196640 | tf_op jit(solution)/shard_map/ppermute | solution.py:160
  153.0 2.3 %collective-permute-start.13 = (bf16[128,1536]{1,0:T(8,128)(2,1)S(1)}, bf16[128,1536]{1,0:T(8,128)(2,1)S(1)}, u32[]{:S(2)}, u32[]{:S(2)}) collective-permute-start(bf16[128,1536]{1,0:T(8,128)(2,1)S(1)} %pad_maximum_fusion.3), channel_id=1, source_target_pairs={{0,32},{32,0},{1,33},{33,1},{2,34},{34,2},{3,35},{35,3},{4,36},{36... | collective-permute-start | bytes 1179656 | tf_op jit(solution)/shard_map/ppermute | solution.py:42
  155.3 4.5 %collective-permute-done.11.refs_4_ = bf16[64,1536]{1,0:T(8,128)(2,1)S(1)} collective-permute-done((bf16[64,1536]{1,0:T(8,128)(2,1)S(1)}, bf16[64,1536]{1,0:T(8,128)(2,1)S(1)}, u32[]{:S(2)}, u32[]{:S(2)}) %collective-permute-start.11) | collective-permute-done | bytes 196640 | tf_op jit(solution)/shard_map/ppermute | solution.py:160
  162.2 7.1 %collective-permute-done.14.refs_11_ = bf16[64,1536]{1,0:T(8,128)(2,1)S(1)} collective-permute-done((bf16[64,1536]{1,0:T(8,128)(2,1)S(1)}, bf16[64,1536]{1,0:T(8,128)(2,1)S(1)}, u32[]{:S(2)}, u32[]{:S(2)}) %collective-permute-start.14) | collective-permute-done | bytes 196640 | tf_op jit(solution)/shard_map/ppermute | solution.py:42
  176.0 4.2 %all-to-all-start.2 = ((bf16[16,32,512]{2,1,0:T(8,128)(2,1)}), bf16[16,32,512]{2,1,0:T(8,128)(2,1)}, u32[]{:S(2)}, u32[]{:S(2)}) async-start(bf16[16,32,512]{2,1,0:T(8,128)(2,1)} %bitcast.15), calls=%async_computation.2 | async-start | bytes 1048576 | tf_op jit(solution)/shard_map/all_to_all | solution.py:264
  185.2 7.0 %weight_gradients.1 = (bf16[512,512]{1,0:T(8,128)(2,1)}, bf16[512,512]{1,0:T(8,128)(2,1)}, bf16[512,512]{1,0:T(8,128)(2,1)}) custom-call(bf16[2,2,128,1024]{3,2,1,0:T(8,128)(2,1)S(1)} %bitcast.12, bf16[2,2,128,1024]{3,2,1,0:T(8,128)(2,1)S(1)} %collective-permute-done.1.other, bf16[64,1536]{1,0:T(8,128)(2,1)S(1)} %hidden_and_grads.1.refs_0_, ...), custom_call_target="tpu_custom_call" | custom-call | flops 1610612736 | bytes 9437184 | tf_op jit(solution)/shard_map/weight_gradients/pallas_call | solution.py:269
  192.3 6.5 %all-to-all-done.2 = bf16[16,32,512]{2,1,0:T(8,128)(2,1)} async-done(((bf16[16,32,512]{2,1,0:T(8,128)(2,1)}), bf16[16,32,512]{2,1,0:T(8,128)(2,1)}, u32[]{:S(2)}, u32[]{:S(2)}) %all-to-all-start.2) | async-done | bytes 524320 | tf_op jit(solution)/shard_map/all_to_all | solution.py:264
  (81 shorter events, 31.3 us)
Async XLA Ops:
  2.5 36.5 %all-to-all-start = ((bf16[16,32,1024]{2,1,0:T(8,128)(2,1)}), bf16[16,32,1024]{2,1,0:T(8,128)(2,1)S(1)}, u32[]{:S(2)}, u32[]{:S(2)}) async-start(bf16[16,32,1024]{2,1,0:T(8,128)(2,1)} %broadcast_in_dim.10), calls=%async_computation | async-start | bytes 2097152 | tf_op jit(solution)/shard_map/all_to_all | solution.py:178
  10.5 22.7 %collective-permute-start = (bf16[1536,512]{1,0:T(8,128)(2,1)S(1)}, bf16[1536,512]{1,0:T(8,128)(2,1)S(1)}, u32[]{:S(2)}, u32[]{:S(2)}) collective-permute-start(bf16[1536,512]{1,0:T(8,128)(2,1)S(1)} %pad_maximum_fusion), channel_id=1, source_target_pairs={{0,64},{1,449},{64,0},{65,129},{128,192},{129,65},{192,128},{193,2... | collective-permute-start | bytes 4718600 | tf_op jit(solution)/shard_map/ppermute | solution.py:156
  39.1 6.4 %collective-permute-start.1 = (bf16[2,2,128,1024]{3,2,1,0:T(8,128)(2,1)S(1)}, bf16[2,2,128,1024]{3,2,1,0:T(8,128)(2,1)S(1)}, u32[]{:S(2)}, u32[]{:S(2)}) collective-permute-start(bf16[2,2,128,1024]{3,2,1,0:T(8,128)(2,1)S(1)} %bitcast.9), channel_id=1, source_target_pairs={{0,1},{1,0},{2,3},{3,2},{4,5},{5,4},{6,7},{7,6},{8,9},{9,8},{10,11... | collective-permute-start | bytes 3145736 | tf_op jit(solution)/shard_map/ppermute | solution.py:42
  42.0 11.2 %collective-permute-start.2 = (bf16[2,128,1024]{2,1,0:T(8,128)(2,1)S(1)}, bf16[2,128,1024]{2,1,0:T(8,128)(2,1)S(1)}, u32[]{:S(2)}, u32[]{:S(2)}) collective-permute-start(bf16[2,128,1024]{2,1,0:T(8,128)(2,1)S(1)} %fusion.1), channel_id=1, source_target_pairs={{0,64},{1,449},{64,0},{65,129},{128,192},{129,65},{192,128},{193,2... | collective-permute-start | bytes 1572872 | tf_op jit(solution)/shard_map/ppermute | solution.py:156
  45.6 13.3 %collective-permute-start.3 = (bf16[2,128,1024]{2,1,0:T(8,128)(2,1)S(1)}, bf16[2,128,1024]{2,1,0:T(8,128)(2,1)S(1)}, u32[]{:S(2)}, u32[]{:S(2)}) collective-permute-start(bf16[2,128,1024]{2,1,0:T(8,128)(2,1)S(1)} %fusion), channel_id=1, source_target_pairs={{0,64},{1,449},{64,0},{65,129},{128,192},{129,65},{192,128},{193,2... | collective-permute-start | bytes 1572872 | tf_op jit(solution)/shard_map/ppermute | solution.py:156
  114.4 7.6 %collective-permute-start.7 = (bf16[64,1536]{1,0:T(8,128)(2,1)S(1)}, bf16[64,1536]{1,0:T(8,128)(2,1)S(1)}, u32[]{:S(2)}, u32[]{:S(2)}) collective-permute-start(bf16[64,1536]{1,0:T(8,128)(2,1)S(1)} %hidden_and_grads.1.refs_0_), channel_id=1, source_target_pairs={{0,448},{64,0},{128,64},{192,128},{256,192},{320,256},{384,320},{4... | collective-permute-start | bytes 589832 | tf_op jit(solution)/shard_map/ppermute | solution.py:160
  117.0 9.5 %collective-permute-start.4 = (bf16[64,1536]{1,0:T(8,128)(2,1)S(1)}, bf16[64,1536]{1,0:T(8,128)(2,1)S(1)}, u32[]{:S(2)}, u32[]{:S(2)}) collective-permute-start(bf16[64,1536]{1,0:T(8,128)(2,1)S(1)} %hidden_and_grads.1.refs_0_), channel_id=1, source_target_pairs={{0,64},{64,128},{128,192},{192,256},{256,320},{320,384},{384,448},... | collective-permute-start | bytes 589832 | tf_op jit(solution)/shard_map/ppermute | solution.py:160
  126.5 44.6 %copy-start.6 = (bf16[64,1536]{1,0:T(8,128)(2,1)}, bf16[64,1536]{1,0:T(8,128)(2,1)S(1)}, u32[]{:S(2)}) copy-start(bf16[64,1536]{1,0:T(8,128)(2,1)S(1)} %collective-permute-done.4.refs_1_) | copy-start | bytes 589828
  126.5 24.6 %collective-permute-start.10 = (bf16[192,1536]{1,0:T(8,128)(2,1)S(1)}, bf16[192,1536]{1,0:T(8,128)(2,1)S(1)}, u32[]{:S(2)}, u32[]{:S(2)}) collective-permute-start(bf16[192,1536]{1,0:T(8,128)(2,1)S(1)} %pad_maximum_fusion.1), channel_id=1, source_target_pairs={{0,32},{32,0},{1,33},{33,1},{2,34},{34,2},{3,35},{35,3},{4,36},{36... | collective-permute-start | bytes 1769480 | tf_op jit(solution)/shard_map/ppermute | solution.py:42
  131.6 7.6 %collective-permute-start.8 = (bf16[64,1536]{1,0:T(8,128)(2,1)S(1)}, bf16[64,1536]{1,0:T(8,128)(2,1)S(1)}, u32[]{:S(2)}, u32[]{:S(2)}) collective-permute-start(bf16[64,1536]{1,0:T(8,128)(2,1)S(1)} %collective-permute-done.7.refs_5_), channel_id=1, source_target_pairs={{0,448},{64,0},{128,64},{192,128},{256,192},{320,256},{384,320},{4... | collective-permute-start | bytes 589832 | tf_op jit(solution)/shard_map/ppermute | solution.py:160
  133.5 8.8 %collective-permute-start.5 = (bf16[64,1536]{1,0:T(8,128)(2,1)S(1)}, bf16[64,1536]{1,0:T(8,128)(2,1)S(1)}, u32[]{:S(2)}, u32[]{:S(2)}) collective-permute-start(bf16[64,1536]{1,0:T(8,128)(2,1)S(1)} %collective-permute-done.4.refs_1_), channel_id=1, source_target_pairs={{0,64},{64,128},{128,192},{192,256},{256,320},{320,384},{384,448},... | collective-permute-start | bytes 589832 | tf_op jit(solution)/shard_map/ppermute | solution.py:160
  139.2 32.0 %copy-start.8 = (bf16[64,1536]{1,0:T(8,128)(2,1)}, bf16[64,1536]{1,0:T(8,128)(2,1)S(1)}, u32[]{:S(2)}) copy-start(bf16[64,1536]{1,0:T(8,128)(2,1)S(1)} %collective-permute-done.8.refs_6_) | copy-start | bytes 589828
  139.2 8.2 %collective-permute-start.9 = (bf16[64,1536]{1,0:T(8,128)(2,1)S(1)}, bf16[64,1536]{1,0:T(8,128)(2,1)S(1)}, u32[]{:S(2)}, u32[]{:S(2)}) collective-permute-start(bf16[64,1536]{1,0:T(8,128)(2,1)S(1)} %collective-permute-done.8.refs_6_), channel_id=1, source_target_pairs={{0,448},{64,0},{128,64},{192,128},{256,192},{320,256},{384,320},{4... | collective-permute-start | bytes 589832 | tf_op jit(solution)/shard_map/ppermute | solution.py:160
  142.3 28.8 %copy-start.10 = (bf16[64,1536]{1,0:T(8,128)(2,1)}, bf16[64,1536]{1,0:T(8,128)(2,1)S(1)}, u32[]{:S(2)}) copy-start(bf16[64,1536]{1,0:T(8,128)(2,1)S(1)} %collective-permute-done.5.refs_2_) | copy-start | bytes 589828
  142.3 8.8 %collective-permute-start.6 = (bf16[64,1536]{1,0:T(8,128)(2,1)S(1)}, bf16[64,1536]{1,0:T(8,128)(2,1)S(1)}, u32[]{:S(2)}, u32[]{:S(2)}) collective-permute-start(bf16[64,1536]{1,0:T(8,128)(2,1)S(1)} %collective-permute-done.5.refs_2_), channel_id=1, source_target_pairs={{0,64},{64,128},{128,192},{192,256},{256,320},{320,384},{384,448},... | collective-permute-start | bytes 589832 | tf_op jit(solution)/shard_map/ppermute | solution.py:160
  145.1 17.1 %collective-permute-start.12 = (bf16[128,1536]{1,0:T(8,128)(2,1)S(1)}, bf16[128,1536]{1,0:T(8,128)(2,1)S(1)}, u32[]{:S(2)}, u32[]{:S(2)}) collective-permute-start(bf16[128,1536]{1,0:T(8,128)(2,1)S(1)} %pad_maximum_fusion.2), channel_id=1, source_target_pairs={{0,32},{32,0},{1,33},{33,1},{2,34},{34,2},{3,35},{35,3},{4,36},{36... | collective-permute-start | bytes 1179656 | tf_op jit(solution)/shard_map/ppermute | solution.py:42
  147.4 23.8 %copy-start.12 = (bf16[64,1536]{1,0:T(8,128)(2,1)}, bf16[64,1536]{1,0:T(8,128)(2,1)S(1)}, u32[]{:S(2)}) copy-start(bf16[64,1536]{1,0:T(8,128)(2,1)S(1)} %collective-permute-done.9.refs_7_) | copy-start | bytes 589828
  151.1 20.1 %copy-start.14 = (bf16[64,1536]{1,0:T(8,128)(2,1)}, bf16[64,1536]{1,0:T(8,128)(2,1)S(1)}, u32[]{:S(2)}) copy-start(bf16[64,1536]{1,0:T(8,128)(2,1)S(1)} %collective-permute-done.6.refs_3_) | copy-start | bytes 589828
  151.1 20.1 %copy-start.16 = (bf16[192,1536]{1,0:T(8,128)(2,1)}, bf16[192,1536]{1,0:T(8,128)(2,1)S(1)}, u32[]{:S(2)}) copy-start(bf16[192,1536]{1,0:T(8,128)(2,1)S(1)} %collective-permute-done.10.refs_8_) | copy-start | bytes 1769476
  151.1 8.8 %collective-permute-start.11 = (bf16[64,1536]{1,0:T(8,128)(2,1)S(1)}, bf16[64,1536]{1,0:T(8,128)(2,1)S(1)}, u32[]{:S(2)}, u32[]{:S(2)}) collective-permute-start(bf16[64,1536]{1,0:T(8,128)(2,1)S(1)} %collective-permute-done.6.refs_3_), channel_id=1, source_target_pairs={{0,64},{64,128},{128,192},{192,256},{256,320},{320,384},{384,448},... | collective-permute-start | bytes 589832 | tf_op jit(solution)/shard_map/ppermute | solution.py:160
  153.0 16.2 %collective-permute-start.13 = (bf16[128,1536]{1,0:T(8,128)(2,1)S(1)}, bf16[128,1536]{1,0:T(8,128)(2,1)S(1)}, u32[]{:S(2)}, u32[]{:S(2)}) collective-permute-start(bf16[128,1536]{1,0:T(8,128)(2,1)S(1)} %pad_maximum_fusion.3), channel_id=1, source_target_pairs={{0,32},{32,0},{1,33},{33,1},{2,34},{34,2},{3,35},{35,3},{4,36},{36... | collective-permute-start | bytes 1179656 | tf_op jit(solution)/shard_map/ppermute | solution.py:42
  159.9 9.4 %collective-permute-start.14 = (bf16[64,1536]{1,0:T(8,128)(2,1)S(1)}, bf16[64,1536]{1,0:T(8,128)(2,1)S(1)}, u32[]{:S(2)}, u32[]{:S(2)}) collective-permute-start(bf16[64,1536]{1,0:T(8,128)(2,1)S(1)} %collective-permute-done.11.refs_4_), channel_id=1, source_target_pairs={{0,32},{32,0},{1,33},{33,1},{2,34},{34,2},{3,35},{35,3},{4,36},{36... | collective-permute-start | bytes 589832 | tf_op jit(solution)/shard_map/ppermute | solution.py:42
  171.2 3.8 %collective-permute-start.15 = (bf16[512,512]{1,0:T(8,128)(2,1)S(1)}, bf16[512,512]{1,0:T(8,128)(2,1)S(1)}, u32[]{:S(2)}, u32[]{:S(2)}) collective-permute-start(bf16[512,512]{1,0:T(8,128)(2,1)S(1)} %get-tuple-element.20), channel_id=1, source_target_pairs={{0,1},{1,0},{2,3},{3,2},{4,5},{5,4},{6,7},{7,6},{8,9},{9,8},{10,11... | collective-permute-start | bytes 1572872 | tf_op jit(solution)/shard_map/ppermute | solution.py:42
  176.0 22.7 %all-to-all-start.2 = ((bf16[16,32,512]{2,1,0:T(8,128)(2,1)}), bf16[16,32,512]{2,1,0:T(8,128)(2,1)}, u32[]{:S(2)}, u32[]{:S(2)}) async-start(bf16[16,32,512]{2,1,0:T(8,128)(2,1)} %bitcast.15), calls=%async_computation.2 | async-start | bytes 1048576 | tf_op jit(solution)/shard_map/all_to_all | solution.py:264
  (20 other events, 117.4 us)
